TPU v7x, 1024 devices: a whole 8x8x8 slice. The times are simulated.
1024 devices in a mesh: sect: 16 (over x_hi, z), blk: 64 (over x_lo, y, core).
Axes of the slice: x: 8 (x_hi: 2, x_lo: 4; x = x_hi * 4 + x_lo), y: 8, z: 8, core: 2. Of those that a mesh axis runs over, the one named last changes fastest.
Arguments:
- fields: float32 [5, 32, 512, 128], P(None, 'sect', 'blk'), may hold values from -6 to 6
- history: bfloat16 [246, 32, 512, 128], P(None, 'sect', 'blk'), may hold values from -800 to 800
- levels: int32 [16, 64], P('sect', 'blk'), may hold values from 0 to 1
- diffusivity: float32 [5], replicated, may hold values from 0.03 to 0.15
- coupling: float32 [5, 5], replicated, may hold values from -1.75 to 1.75
Outputs:
- pod_modes: float32 [256, 32, 512, 128], P(None, 'sect', 'blk')
- factor: float32 [256, 256], replicated
All inputs are finite; a program needn't handle non-finite values.
Results may differ from a plain program's by a relative error of at most 0.0003.
Values sent between devices are 32-bit elements; how exact they have to be, the bound alone decides.
A program may use at most 128 MiB of HBM per device.

v0:
```python
import jax
import jax.numpy as jnp
from jax import lax
from jax.sharding import PartitionSpec as P


def extended_2(cells, sides, width):
    for axis, dim in sides:
        count = lax.axis_size(axis)
        ends = count - 1
        head = lax.slice_in_dim(cells, 0, width, axis=dim)
        tail = lax.slice_in_dim(cells, cells.shape[dim] - width, cells.shape[dim], axis=dim)
        cells = jnp.concatenate(
            [
                lax.ppermute(tail, axis, [(i, (i + 1) % count) for i in range(ends)]),
                cells,
                lax.ppermute(head, axis, [((i + 1) % count, i) for i in range(ends)]),
            ],
            axis=dim,
        )
    return cells


def tendency(current, diffusivity, coupling):
    extended = extended_2(current, (("sect", 1), ("blk", 2)), 1)
    padded = jnp.pad(extended, ((0, 0), (0, 0), (0, 0), (1, 1)))
    center = padded[:, 1:-1, 1:-1, 1:-1]
    beside_all = padded[:, 2:, 1:-1, 1:-1] + padded[:, :-2, 1:-1, 1:-1]
    beside_all = beside_all + padded[:, 1:-1, 2:, 1:-1] + padded[:, 1:-1, :-2, 1:-1]
    beside_all = beside_all + padded[:, 1:-1, 1:-1, 2:] + padded[:, 1:-1, 1:-1, :-2]
    beside_all = beside_all - 6.0 * center
    coupled = jnp.einsum("fg,gxyz->fxyz", coupling, current, precision=lax.Precision.HIGHEST)
    return diffusivity[:, None, None, None] * beside_all + coupled


def shards(fields, history, levels, diffusivity, coupling):
    refined = levels[0, 0].astype(jnp.float32)
    stride = 1.0 / (1.0 + refined)
    first_state = fields + stride * tendency(fields, diffusivity, coupling)
    final_state = first_state + refined * stride * tendency(first_state, diffusivity, coupling)
    change = final_state - fields
    stored_count, count_x, count_y, count_z = history.shape
    local_rows = count_x * count_y * count_z
    snapshot = jnp.concatenate([history.astype(jnp.float32), final_state, change], axis=0)
    snapshot = snapshot.reshape(-1, local_rows)
    gram_local = jnp.dot(snapshot, snapshot.T, precision=lax.Precision.HIGHEST)
    total_rows = local_rows * lax.axis_size("sect") * lax.axis_size("blk")
    gram_total = lax.psum(gram_local, ("sect", "blk"))
    upper_tri = jnp.linalg.cholesky(gram_total).T
    factor = upper_tri / jnp.sqrt(jnp.float32(total_rows))
    solved = lax.linalg.triangular_solve(factor.T, snapshot, left_side=True, lower=True)
    pod_modes = solved.reshape(-1, count_x, count_y, count_z)
    return (pod_modes, factor)


def solution(mesh):
    return jax.shard_map(
        shards,
        mesh=mesh,
        in_specs=(
            P(None, "sect", "blk", None),
            P(None, "sect", "blk", None),
            P("sect", "blk"),
            P(),
            P(),
        ),
        out_specs=(P(None, "sect", "blk", None), P()),
        check_vma=False,
    )
```

profile of v0, /device:TPU:1, one launch (start us, length us, event | category | flops | bytes accessed | tf_op | source)
XLA Modules:
  0.0 428.1 jit_solution(2651913122847029889)
XLA Ops:
  7.2 0.0 all-reduce.5.cloned.1.call-start
  7.2 0.8 fusion.44
  8.0 5.7 %collective-permute-start.1 = (f32[5,1,8,128]{3,2,1,0:T(8,128)S(1)}, f32[5,1,8,128]{3,2,1,0:T(8,128)S(1)}, u32[]{:S(2)}, u32[]{:S(2)}) collective-permute-start(f32[5,1,8,128]{3,2,1,0:T(8,128)S(1)} %get-tuple-element.41), channel_id=1, source_target_pairs={{0,64},{64,128},{128,192},{192,256},{256,320},{320,384},{384,448},... | collective-permute-start | bytes 61448 | tf_op jit(solution)/shard_map/ppermute | solution.py:15
  13.7 1.3 collective-permute-start
  15.0 0.8 constant_dynamic-update-slice_fusion.1
  15.8 4.0 collective-permute-done
  19.8 11.2 %collective-permute-start.2 = (f32[5,4,1,128]{3,2,1,0:T(1,128)S(1)}, f32[5,4,1,128]{3,2,1,0:T(1,128)S(1)}, u32[]{:S(2)}, u32[]{:S(2)}) collective-permute-start(f32[5,4,1,128]{3,2,1,0:T(1,128)S(1)} %get-tuple-element.33), channel_id=1, source_target_pairs={{1,0},{2,1},{3,2},{4,3},{5,4},{6,5},{7,6},{8,7},{9,8},{10,9},{11,1... | collective-permute-start | bytes 30728 | tf_op jit(solution)/shard_map/ppermute | solution.py:17
  31.0 1.9 collective-permute-start.3
  33.0 1.0 fusion.19
  34.7 0.2 select_maximum_fusion.4
  34.9 1.0 fusion.33
  35.9 1.3 collective-permute-start.4
  37.2 4.0 collective-permute-start.5
  41.2 1.4 convert_element_type.12
  42.6 3.0 collective-permute-start.6
  45.7 2.8 collective-permute-start.7
  48.5 0.2 fusion.17
  48.7 0.6 collective-permute-done.7
  49.3 0.2 select_maximum_fusion
  49.5 0.1 fusion.39
  49.6 0.1 pad_maximum_fusion
  49.8 3.6 fusion.2
  53.4 0.0 all-reduce.5.cloned.1.call-update
  53.4 0.1 triangular_solve.79
  53.5 0.4 copy.42
  53.9 0.3 copy.43
  54.3 299.9 %all-reduce.5.cloned.1.call-done = f32[256,256]{0,1:T(8,128)} async-done(((f32[256,256]{0,1:T(8,128)}), f32[256,256]{0,1:T(8,128)}) %all-reduce.5.cloned.1.call-update) | async-done | bytes 262160 | tf_op jit(solution)/shard_map/psum | solution.py:48
  354.2 1.1 copy.41
  355.3 1.0 fusion.9
  356.3 11.7 %cholesky.50 = f32[128,128]{1,0:T(8,128)S(1)} custom-call(f32[128,128]{1,0:T(8,128)S(1)} %cholesky.118), custom_call_target="Cholesky" | custom-call | tf_op jit(solution)/shard_map/jit(cholesky)/cholesky | solution.py:49
  368.0 9.8 %custom-call.14 = f32[1,128,128]{1,2,0:T(8,128)S(1)} custom-call(f32[1,128,128]{2,1,0:T(8,128)S(1)} %get-tuple-element.37), custom_call_target="InvertDiagBlocksLowerTriangular" | custom-call | tf_op jit(solution)/shard_map/jit(cholesky)/cholesky | solution.py:49
  377.9 0.2 constant_dynamic-update-slice_fusion.4
  378.1 0.3 convolution_subtract_fusion.1
  378.3 11.9 %cholesky.105 = f32[128,128]{1,0:T(8,128)S(1)} custom-call(f32[128,128]{1,0:T(8,128)S(1)} %convolution_subtract_fusion.1), custom_call_target="Cholesky" | custom-call | tf_op jit(solution)/shard_map/jit(cholesky)/cholesky | solution.py:49
  390.3 0.6 compare_reduce_fusion
  392.2 0.1 triangular_solve.61
  392.2 3.8 while.1
  392.2 0.6 fusion.50
  392.8 1.3 bitcast_dynamic-update-slice_fusion.2
  394.2 0.6 fusion.50
  394.7 1.3 bitcast_dynamic-update-slice_fusion.2
  396.1 19.7 %custom-call.15 = f32[2,128,128]{1,2,0:T(8,128)S(1)} custom-call(f32[2,128,128]{2,1,0:T(8,128)S(1)} %get-tuple-element.9), custom_call_target="InvertDiagBlocksLowerTriangular" | custom-call | tf_op jit(solution)/shard_map/triangular_solve | solution.py:51
  415.8 0.6 fusion.5
  416.4 1.0 convolution_subtract_fusion
  417.4 1.1 fusion.13
  418.5 0.2 maximum_bitcast_fusion
  418.7 1.7 copy.49
  420.4 0.8 copy.44
  (28 shorter events, 0.2 us)
Async XLA Ops:
  7.2 25.8 %copy-start = (f32[5,5]{1,0:T(8,128)S(1)}, f32[5,5]{1,0:T(8,128)}, u32[]{:S(2)}) copy-start(f32[5,5]{1,0:T(8,128)} %param.9) | copy-start | bytes 304
  7.2 347.0 %all-reduce.5.cloned.1.call-start = ((), (), s32[]{:S(2)}) async-start(), calls=%async_computation | async-start | bytes 524288 | tf_op jit(solution)/shard_map/psum | solution.py:48
  8.0 7.0 %collective-permute-start.1 = (f32[5,1,8,128]{3,2,1,0:T(8,128)S(1)}, f32[5,1,8,128]{3,2,1,0:T(8,128)S(1)}, u32[]{:S(2)}, u32[]{:S(2)}) collective-permute-start(f32[5,1,8,128]{3,2,1,0:T(8,128)S(1)} %get-tuple-element.41), channel_id=1, source_target_pairs={{0,64},{64,128},{128,192},{192,256},{256,320},{320,384},{384,448},... | collective-permute-start | bytes 61448 | tf_op jit(solution)/shard_map/ppermute | solution.py:15
  13.7 6.1 %collective-permute-start = (f32[5,1,8,128]{3,2,1,0:T(8,128)S(1)}, f32[5,1,8,128]{3,2,1,0:T(8,128)S(1)}, u32[]{:S(2)}, u32[]{:S(2)}) collective-permute-start(f32[5,1,8,128]{3,2,1,0:T(8,128)S(1)} %get-tuple-element.40), channel_id=1, source_target_pairs={{64,0},{128,64},{192,128},{256,192},{320,256},{384,320},{448,384},... | collective-permute-start | bytes 61448 | tf_op jit(solution)/shard_map/ppermute | solution.py:17
  19.8 14.8 %collective-permute-start.2 = (f32[5,4,1,128]{3,2,1,0:T(1,128)S(1)}, f32[5,4,1,128]{3,2,1,0:T(1,128)S(1)}, u32[]{:S(2)}, u32[]{:S(2)}) collective-permute-start(f32[5,4,1,128]{3,2,1,0:T(1,128)S(1)} %get-tuple-element.33), channel_id=1, source_target_pairs={{1,0},{2,1},{3,2},{4,3},{5,4},{6,5},{7,6},{8,7},{9,8},{10,9},{11,1... | collective-permute-start | bytes 30728 | tf_op jit(solution)/shard_map/ppermute | solution.py:17
  31.0 3.6 collective-permute-start.3
  34.9 14.6 %copy-start.1 = (f32[5,2,8,128]{3,2,1,0:T(8,128)S(1)}, f32[5,2,8,128]{3,2,1,0:T(8,128)}, u32[]{:S(2)}) copy-start(f32[5,2,8,128]{3,2,1,0:T(8,128)} %param.5) | copy-start | bytes 122884
  34.9 14.6 %copy-start.2 = (f32[5]{0:T(128)S(1)}, f32[5]{0:T(128)}, u32[]{:S(2)}) copy-start(f32[5]{0:T(128)} %param.8) | copy-start | bytes 64
  35.9 6.7 %collective-permute-start.4 = (f32[5,1,8,128]{3,2,1,0:T(8,128)S(1)}, f32[5,1,8,128]{3,2,1,0:T(8,128)S(1)}, u32[]{:S(2)}, u32[]{:S(2)}) collective-permute-start(f32[5,1,8,128]{3,2,1,0:T(8,128)S(1)} %get-tuple-element.39), channel_id=1, source_target_pairs={{64,0},{128,64},{192,128},{256,192},{320,256},{384,320},{448,384},... | collective-permute-start | bytes 61448 | tf_op jit(solution)/shard_map/ppermute | solution.py:17
  37.2 5.4 %collective-permute-start.5 = (f32[5,1,8,128]{3,2,1,0:T(8,128)S(1)}, f32[5,1,8,128]{3,2,1,0:T(8,128)S(1)}, u32[]{:S(2)}, u32[]{:S(2)}) collective-permute-start(f32[5,1,8,128]{3,2,1,0:T(8,128)S(1)} %get-tuple-element.38), channel_id=1, source_target_pairs={{0,64},{64,128},{128,192},{192,256},{256,320},{320,384},{384,448},... | collective-permute-start | bytes 61448 | tf_op jit(solution)/shard_map/ppermute | solution.py:15
  42.6 6.0 %collective-permute-start.6 = (f32[5,4,1,128]{3,2,1,0:T(1,128)S(1)}, f32[5,4,1,128]{3,2,1,0:T(1,128)S(1)}, u32[]{:S(2)}, u32[]{:S(2)}) collective-permute-start(f32[5,4,1,128]{3,2,1,0:T(1,128)S(1)} %get-tuple-element.31), channel_id=1, source_target_pairs={{1,0},{2,1},{3,2},{4,3},{5,4},{6,5},{7,6},{8,7},{9,8},{10,9},{11,1... | collective-permute-start | bytes 30728 | tf_op jit(solution)/shard_map/ppermute | solution.py:17
  45.7 3.6 collective-permute-start.7
  54.3 361.5 %slice-start = ((bf16[246,2,8,128]{3,2,1,0:T(8,128)(2,1)}), bf16[128,2,8,128]{3,2,1,0:T(8,128)(2,1)S(1)}, s32[]{:S(2)}) async-start(bf16[246,2,8,128]{3,2,1,0:T(8,128)(2,1)} %param.6), calls=%async_computation.1 | async-start | bytes 1048576 | tf_op jit(solution)/shard_map/triangular_solve | solution.py:51
Sparse Core Ops, SparseCore 0:
  53.5 300.5 all-reduce.4
where the time goes:
time: 429 us; the launch traced here: 428 us
  waiting for transfers between devices  304 us (71%)
  other arithmetic  58.1 us (14%)
  starting transfers between devices  31.3 us (7%)
  between operations  16.3 us (4%)
  local copies, waits for them, and re-layouts  9.9 us (2%)
  matrix products  7.97 us (2%)
    psum x1, waiting for transfers between devices, shards(): gram_total = lax.psum(gram_local, ('sect', 'blk'))  300 us
    another operation x6, other arithmetic, shards(): upper_tri = jnp.linalg.cholesky(gram_total).T  34.1 us
    another operation x2, other arithmetic, shards(): lax.linalg.triangular_solve(factor.T, snapshot, left_side=True, lower=True)  19.7 us
    ppermute x4, starting transfers between devices, extended_2(): lax.ppermute(head, axis, [((i + 1) % count, i) for i in range(ends)])  16.8 us
    ppermute x4, starting transfers between devices, extended_2(): lax.ppermute(tail, axis, [(i, (i + 1) % count) for i in range(ends)])  14.4 us
  transfers between devices with their start and end apart: 9, of which 3 were waited for; matrix products, arithmetic and copies ran while one was open for 1% of the time, Pallas kernels for 0%

commit v1 on v0

v1 whole, which is shorter than its diff:
```python
import functools
import math

import jax
import jax.numpy as jnp
from jax import lax
from jax.experimental import pallas as pl
from jax.experimental.pallas import tpu as pltpu
from jax.sharding import PartitionSpec as P

F32 = jnp.float32
BF16 = jnp.bfloat16
MESH = pl.DeviceIdType.MESH
Z_CHIPS = 8
Y_CHIPS = 8
X_LOW = 4
RING = 8
BLOCK = 32
GROUP = 16


def position():
    sect = lax.axis_index("sect")
    blk = lax.axis_index("blk")
    x = (sect // Z_CHIPS) * X_LOW + blk // (2 * Y_CHIPS)
    y = (blk // 2) % Y_CHIPS
    return x, y, sect % Z_CHIPS, blk % 2


def device(x, y, z, core):
    return ((x // X_LOW) * Z_CHIPS + z, ((x % X_LOW) * Y_CHIPS + y) * 2 + core)


def neighbour_sum(cells, sect_low, sect_high, blk_low, blk_high, sub, lane):
    out = []
    for f in range(len(cells)):
        row = []
        for x in range(2):
            c = cells[f][x]
            low = sect_low[f] if x == 0 else cells[f][0]
            high = sect_high[f] if x == 1 else cells[f][1]
            up = jnp.where(sub == 0, jnp.broadcast_to(blk_low[2 * f + x], (8, 128)), pltpu.roll(c, 1, 0))
            down = jnp.where(sub == 7, jnp.broadcast_to(blk_high[2 * f + x], (8, 128)), pltpu.roll(c, 7, 0))
            left = jnp.where(lane == 0, 0.0, pltpu.roll(c, 1, 1))
            right = jnp.where(lane == 127, 0.0, pltpu.roll(c, 127, 1))
            row.append(((high + low) + (down + up) + (right + left)) - 6.0 * c)
        out.append(row)
    return out


def tendency(cells, beside, diffusivity, coupling):
    count = len(cells)
    out = []
    for f in range(count):
        row = []
        for x in range(2):
            total = coupling[f, 0] * cells[0][x]
            for g in range(1, count):
                total = total + coupling[f, g] * cells[g][x]
            row.append(diffusivity[f] * beside[f][x] + total)
        out.append(row)
    return out


def split3(x):
    high = x.astype(BF16)
    rest = x - high.astype(F32)
    mid = rest.astype(BF16)
    low = (rest - mid.astype(F32)).astype(BF16)
    return high, mid, low


def dot_rows(a, b):
    return lax.dot_general(a, b, (((1,), (1,)), ((), ())), preferred_element_type=F32)


def dot_columns(a, b):
    return lax.dot_general(a, b, (((0,), (0,)), ((), ())), preferred_element_type=F32)


def gather_kernel(
    edges,
    hist_ref, fields_ref, levels_ref, diff_ref, coup_ref,
    gram_ref, snap_out, fine_out,
    hist, wide, snap, fine,
    edge_sect, edge_blk, stage_blk, stage_sect,
    h_send, h_half, h_slots, h_part, h_final,
    f_send, f_half, f_slots, f_part, f_final,
    local_sem, send_sem, recv_sem,
):
    n_sect, n_blk = edges
    sect = lax.axis_index("sect")
    blk = lax.axis_index("blk")
    x, y, z, core = position()
    other = device(x, y, z, 1 - core)
    along_x = [device((x + k) % RING, y, z, core) for k in range(1, RING)]
    along_y = [device(x, (y + k) % RING, z, core) for k in range(1, RING)]
    along_z = [device(x, y, (z + k) % RING, core) for k in range(1, RING)]
    sect_down = ((sect + n_sect - 1) % n_sect, blk)
    sect_up = ((sect + 1) % n_sect, blk)
    blk_down = (sect, (blk + n_blk - 1) % n_blk)
    blk_up = (sect, (blk + 1) % n_blk)
    peers = [other] + along_x + along_y + along_z + [sect_down, sect_up, blk_down, blk_up]

    load = pltpu.make_async_copy(hist_ref, hist, local_sem.at[0])
    load.start()
    barrier = pltpu.get_barrier_semaphore()
    for peer in peers:
        pl.semaphore_signal(barrier, inc=1, device_id=peer, device_id_type=MESH)

    def send(src, dst, index, target):
        pltpu.make_async_remote_copy(
            src_ref=src, dst_ref=dst, send_sem=send_sem.at[index], recv_sem=recv_sem.at[index],
            device_id=target, device_id_type=MESH,
        ).start()

    def wait_recv(ref, index):
        pltpu.make_async_copy(ref, ref, recv_sem.at[index]).wait()

    def wait_send(ref, index):
        pltpu.make_async_copy(ref, ref, send_sem.at[index]).wait()

    sub = lax.broadcasted_iota(jnp.int32, (8, 128), 0)
    lane = lax.broadcasted_iota(jnp.int32, (8, 128), 1)
    count = fields_ref.shape[0]
    stored = hist_ref.shape[0]
    columns = stored + 2 * count
    half_columns = columns // 2

    load.wait()
    wide[0:stored * 16, :] = hist[...].astype(F32).reshape(stored * 16, 128)
    wide[stored * 16:, :] = jnp.zeros((2 * count * 16, 128), F32)
    for q in range(16):
        snap[:, 128 * q:128 * q + 128] = wide[pl.ds(q, columns, stride=16), :].astype(BF16)
    gram = dot_rows(snap[...], snap[...])
    i = lax.broadcasted_iota(jnp.int32, (128, 128), 0)
    j = lax.broadcasted_iota(jnp.int32, (128, 128), 1)
    corner = gram[128:, 128:]
    diagonal = jnp.sum(jnp.where(i == j, corner, 0.0), axis=0, keepdims=True)
    folded = jnp.where(i <= j, gram[:128, :128], corner)
    folded = jnp.where((i == 127) & (j < 112), diagonal, folded)
    h_send[0] = folded.reshape(RING, 16, 128)
    h_send[1] = gram[:128, 128:].reshape(RING, 16, 128)

    cells = [[fields_ref[f, k] for k in range(2)] for f in range(count)]

    def send_edges(values, first):
        for f in range(count):
            for k in range(2):
                if first == 1:
                    stage_sect[k, f] = values[f][k]
                stage_blk[first, 0, 2 * f + k:2 * f + k + 1, :] = values[f][k][0:1, :]
                stage_blk[first, 1, 2 * f + k:2 * f + k + 1, :] = values[f][k][7:8, :]
        low = fields_ref.at[:, 0] if first == 0 else stage_sect.at[0]
        high = fields_ref.at[:, 1] if first == 0 else stage_sect.at[1]
        send(low, edge_sect.at[first, 1], 2 * first, sect_down)
        send(high, edge_sect.at[first, 0], 2 * first, sect_up)
        send(stage_blk.at[first, 0], edge_blk.at[first, 1], 2 * first + 1, blk_down)
        send(stage_blk.at[first, 1], edge_blk.at[first, 0], 2 * first + 1, blk_up)

    def take_edges(first):
        wait_recv(edge_sect.at[first], 2 * first)
        wait_recv(edge_blk.at[first], 2 * first + 1)
        sect_low = [jnp.where(sect == 0, 0.0, edge_sect[first, 0, f]) for f in range(count)]
        sect_high = [jnp.where(sect == n_sect - 1, 0.0, edge_sect[first, 1, f]) for f in range(count)]
        blk_low = [jnp.where(blk == 0, 0.0, edge_blk[first, 0, r:r + 1, :]) for r in range(2 * count)]
        blk_high = [jnp.where(blk == n_blk - 1, 0.0, edge_blk[first, 1, r:r + 1, :]) for r in range(2 * count)]
        return sect_low, sect_high, blk_low, blk_high

    pl.semaphore_wait(barrier, len(peers))
    send_edges(cells, 0)
    send(h_send.at[1 - core], h_half.at[0], 4, other)

    refined = jnp.zeros((8, 128), jnp.int32) + levels_ref[0, 0]
    refined = refined.astype(F32)
    stride = 1.0 / (1.0 + refined)

    wait_recv(h_half.at[0], 4)
    h_half[1] = h_send[core] + h_half[0]
    for k in range(1, RING):
        send(h_half.at[1, (y + k) % RING], h_slots.at[0, k - 1], 5, along_y[k - 1])

    beside = neighbour_sum(cells, *take_edges(0), sub, lane)
    tend = tendency(cells, beside, diff_ref, coup_ref)
    first_state = [[cells[f][k] + stride * tend[f][k] for k in range(2)] for f in range(count)]
    send_edges(first_state, 1)

    wait_recv(h_slots.at[0], 5)
    total = h_half[1, y]
    for k in range(RING - 1):
        total = total + h_slots[0, k]
    h_part[0] = total
    for k in range(1, RING):
        send(h_part.at[0], h_slots.at[1, k - 1], 6, along_x[k - 1])

    beside = neighbour_sum(first_state, *take_edges(1), sub, lane)
    tend = tendency(first_state, beside, diff_ref, coup_ref)
    weight = refined * stride
    for f in range(count):
        for k in range(2):
            final = first_state[f][k] + weight * tend[f][k]
            row = (stored + f) * 16 + 8 * k
            wide[row:row + 8, :] = final
            row = (stored + count + f) * 16 + 8 * k
            wide[row:row + 8, :] = final - cells[f][k]
    for q in range(16):
        high, mid, low = split3(wide[pl.ds((columns - 16) * 16 + q, 16, stride=16), :])
        snap[columns - 16:columns, 128 * q:128 * q + 128] = high
        fine[0, :, 128 * q:128 * q + 128] = mid
        fine[1, :, 128 * q:128 * q + 128] = low
    keep_snap = pltpu.make_async_copy(snap, snap_out, local_sem.at[1])
    keep_snap.start()
    keep_fine = pltpu.make_async_copy(fine, fine_out, local_sem.at[2])
    keep_fine.start()
    pieces = jnp.concatenate([snap[columns - 16:columns, :], fine[0], fine[1]], axis=0)
    fresh = dot_rows(pieces, snap[...])
    fresh_fine = dot_rows(pieces, pieces[16:])
    fresh = fresh[0:16] + fresh[16:32] + fresh[32:48]
    extra = fresh_fine[0:16, 0:16] + (fresh_fine[0:16, 16:32] + fresh_fine[16:32, 0:16])
    f_send[0] = fresh[:, :half_columns]
    f_send[1] = fresh[:, half_columns:]
    f_send[1, :, half_columns - 16:] = fresh[:, columns - 16:] + extra
    send(f_send.at[1 - core], f_half.at[0], 7, other)

    wait_recv(f_half.at[0], 7)
    f_part[0] = f_send[core] + f_half[0]
    for k in range(1, RING):
        send(f_part.at[0], f_slots.at[0, k - 1], 8, along_x[k - 1])

    wait_recv(h_slots.at[1], 6)
    total = h_part[0]
    for k in range(RING - 1):
        total = total + h_slots[1, k]
    h_part[1] = total
    for k in range(1, RING):
        send(h_part.at[1], h_slots.at[2, k - 1], 9, along_z[k - 1])

    wait_recv(f_slots.at[0], 8)
    total = f_part[0]
    for k in range(RING - 1):
        total = total + f_slots[0, k]
    f_part[1] = total
    for k in range(1, RING):
        send(f_part.at[1], f_slots.at[1, k - 1], 10, along_z[k - 1])

    wait_recv(h_slots.at[2], 9)
    total = h_part[1]
    for k in range(RING - 1):
        total = total + h_slots[2, k]
    h_final[core, y] = total
    for k in range(1, RING):
        send(h_final.at[core, y], h_final.at[core, y], 11, along_y[k - 1])

    wait_recv(f_slots.at[1], 10)
    total = f_part[1]
    for k in range(RING - 1):
        total = total + f_slots[1, k]
    f_part[2] = total
    for k in range(1, RING):
        send(f_part.at[2], f_slots.at[2, k - 1], 12, along_y[k - 1])

    wait_recv(h_slots.at[2], 11)
    send(h_final.at[core], h_final.at[core], 13, other)

    wait_recv(f_slots.at[2], 12)
    total = f_part[2]
    for k in range(RING - 1):
        total = total + f_slots[2, k]
    f_final[core] = total
    send(f_final.at[core], f_final.at[core], 14, other)

    wait_recv(h_final.at[0], 13)
    wait_recv(f_final.at[0], 14)

    folded = h_final[0].reshape(128, 128)
    turned = folded.T
    first = jnp.where(i <= j, folded, turned)
    corner = jnp.where(i > j, folded, turned)
    corner = jnp.where(i == j, jnp.broadcast_to(folded[127:128, :], (128, 128)), corner)
    side = h_final[1].reshape(128, 128)
    low_rows = jnp.concatenate([jnp.zeros((112, 128), F32), f_final[0]], axis=0).T
    high_rows = jnp.concatenate([jnp.zeros((112, 128), F32), f_final[1]], axis=0)
    corner = jnp.where(i >= 112, high_rows, jnp.where(j >= 112, high_rows.T, corner))
    side = jnp.where(j >= 112, low_rows, side)
    gram_ref[0:128, 0:128] = first
    gram_ref[0:128, 128:] = side
    gram_ref[128:, 0:128] = side.T
    gram_ref[128:, 128:] = corner

    for first_round in range(2):
        wait_send(edge_sect.at[first_round], 2 * first_round)
        wait_send(edge_blk.at[first_round], 2 * first_round + 1)
    wait_send(h_half.at[0], 4)
    wait_send(h_slots.at[0], 5)
    wait_send(h_slots.at[0], 6)
    wait_send(f_half.at[0], 7)
    wait_send(f_slots.at[0], 8)
    wait_send(h_slots.at[0], 9)
    wait_send(f_slots.at[0], 10)
    wait_send(h_slots.at[0], 11)
    wait_send(f_slots.at[0], 12)
    wait_send(h_final.at[0], 13)
    wait_send(f_final.at[0], 14)
    keep_snap.wait()
    keep_fine.wait()


def eliminate(rows, col0, width):
    count = BLOCK // 8
    tiles = width // 128
    values = [rows[8 * v:8 * v + 8] for v in range(count)]
    pivots = [jnp.zeros((8, 128), F32) for _ in range(count)]
    sub = lax.broadcasted_iota(jnp.int32, (8, 128), 0)
    for start in range(0, BLOCK, GROUP):
        v0 = start // 8
        spread = [
            [jnp.broadcast_to(values[v][:, col0 + start + p:col0 + start + p + 1], (8, 128)) for v in range(v0, count)]
            for p in range(GROUP)
        ]
        for p in range(GROUP):
            vp, s = (start + p) // 8, (start + p) % 8
            raw = spread[p]
            pivot = jnp.broadcast_to(raw[vp - v0][s:s + 1, :], (8, 128))
            inverse = 1.0 / pivot
            pivots[vp] = jnp.where(sub == s, pivot, pivots[vp])
            factors = {}
            for v in range(vp, count):
                factor = raw[v - v0] * inverse
                factors[v] = jnp.where(sub > s, factor, 0.0) if v == vp else factor
            for later in range(p + 1, GROUP):
                vl, sl = (start + later) // 8, (start + later) % 8
                across = jnp.broadcast_to(raw[vl - v0][sl:sl + 1, :], (8, 128))
                for v in range(vp, count):
                    spread[later][v - v0] = spread[later][v - v0] - factors[v] * across
            row = jnp.broadcast_to(values[vp][s:s + 1, :], (8, width))
            for v in range(vp, count):
                if v == vp and s == 7:
                    continue
                values[v] = values[v] - jnp.concatenate([factors[v]] * tiles, axis=1) * row
    return jnp.concatenate(
        [values[v] * jnp.concatenate([lax.rsqrt(pivots[v])] * tiles, axis=1) for v in range(count)], axis=0
    )


def finish_kernel(
    total_rows,
    gram_ref, snap_ref, fine_ref,
    modes_ref, factor_ref,
    work, inverse, snap, fine, modes, local_sem,
):
    size = gram_ref.shape[0]
    load_snap = pltpu.make_async_copy(snap_ref, snap, local_sem.at[0])
    load_snap.start()
    load_fine = pltpu.make_async_copy(fine_ref, fine, local_sem.at[1])
    load_fine.start()
    scale = math.sqrt(total_rows)
    shape = (size, size)
    identity = lax.broadcasted_iota(jnp.int32, shape, 0) == lax.broadcasted_iota(jnp.int32, shape, 1)
    work[:, :size] = gram_ref[...]
    work[:, size:] = identity.astype(F32)
    rows = work[0:BLOCK, :]
    for b0 in range(0, size, BLOCK):
        done = eliminate(rows, b0, 2 * size)
        i = lax.broadcasted_iota(jnp.int32, (BLOCK, size), 0) + b0
        j = lax.broadcasted_iota(jnp.int32, (BLOCK, size), 1)
        upper = jnp.where(j >= i, done[:, :size], 0.0)
        factor_ref[b0:b0 + BLOCK, :] = upper * (1.0 / scale)
        inverse[b0:b0 + BLOCK, :] = done[:, size:] * scale
        b1 = b0 + BLOCK
        if b1 < size:
            h, m, l = split3(upper)
            left = jnp.concatenate([h, h, m, m, h, l], axis=0)
            h, m, l = split3(done)
            right = jnp.concatenate([h, m, h, m, l, h], axis=0)
            rows = work[b1:b1 + BLOCK, :] - dot_columns(left[:, b1:b1 + BLOCK], right)
            if b1 + BLOCK < size:
                work[b1 + BLOCK:, :] = work[b1 + BLOCK:, :] - dot_columns(left[:, b1 + BLOCK:], right)
    load_snap.wait()
    load_fine.wait()
    step = 64
    stores = []
    tail = jnp.concatenate([fine[0], fine[0], fine[0], fine[1]], axis=0)
    for r0 in range(0, size, step):
        h, m, l = split3(inverse[r0:r0 + step, :])
        out = jnp.dot(h, snap[...], preferred_element_type=F32)
        out = out + jnp.dot(m, snap[...], preferred_element_type=F32)
        out = out + jnp.dot(l, snap[...], preferred_element_type=F32)
        last = jnp.concatenate([h[:, size - 16:], m[:, size - 16:], l[:, size - 16:], h[:, size - 16:]], axis=1)
        out = out + jnp.dot(last, tail, preferred_element_type=F32)
        for q in range(16):
            modes[pl.ds(r0 * 16 + q, step, stride=16), :] = out[:, 128 * q:128 * q + 128]
        store = pltpu.make_async_copy(
            modes.at[pl.ds(r0 * 16, step * 16)], modes_ref.at[pl.ds(r0 * 16, step * 16)], local_sem.at[2 + r0 // step]
        )
        store.start()
        stores.append(store)
    for store in stores:
        store.wait()


def shards(fields, history, levels, diffusivity, coupling):
    edges = (lax.axis_size("sect"), lax.axis_size("blk"))
    stored, count_x, count_y, count_z = history.shape
    count = fields.shape[0]
    columns = stored + 2 * count
    local = count_x * count_y * count_z
    vmem = pl.BlockSpec(memory_space=pltpu.VMEM)
    smem = pl.BlockSpec(memory_space=pltpu.SMEM)
    anywhere = pl.BlockSpec(memory_space=pl.ANY)
    gram, snap, fine = pl.pallas_call(
        functools.partial(gather_kernel, edges),
        out_shape=[
            jax.ShapeDtypeStruct((columns, columns), F32),
            jax.ShapeDtypeStruct((columns, local), BF16),
            jax.ShapeDtypeStruct((2, 16, local), BF16),
        ],
        in_specs=[anywhere, vmem, smem, smem, smem],
        out_specs=[vmem, anywhere, anywhere],
        scratch_shapes=[
            pltpu.VMEM(history.shape, BF16),
            pltpu.VMEM((columns * 16, 128), F32),
            pltpu.VMEM((columns, local), BF16),
            pltpu.VMEM((2, 16, local), BF16),
            pltpu.VMEM((2, 2, count, 8, 128), F32),
            pltpu.VMEM((2, 2, 16, 128), F32),
            pltpu.VMEM((2, 2, 16, 128), F32),
            pltpu.VMEM((2, count, 8, 128), F32),
            pltpu.VMEM((2, RING, 16, 128), F32),
            pltpu.VMEM((2, RING, 16, 128), F32),
            pltpu.VMEM((3, RING - 1, 16, 128), F32),
            pltpu.VMEM((2, 16, 128), F32),
            pltpu.VMEM((2, RING, 16, 128), F32),
            pltpu.VMEM((2, 16, 128), F32),
            pltpu.VMEM((1, 16, 128), F32),
            pltpu.VMEM((3, RING - 1, 16, 128), F32),
            pltpu.VMEM((3, 16, 128), F32),
            pltpu.VMEM((2, 16, 128), F32),
            pltpu.SemaphoreType.DMA((3,)),
            pltpu.SemaphoreType.DMA((15,)),
            pltpu.SemaphoreType.DMA((15,)),
        ],
        compiler_params=pltpu.CompilerParams(
            collective_id=0, has_side_effects=True, vmem_limit_bytes=32 << 20
        ),
        name="gather",
    )(history, fields, levels, diffusivity, coupling)
    modes, factor = pl.pallas_call(
        functools.partial(finish_kernel, local * edges[0] * edges[1]),
        out_shape=[
            jax.ShapeDtypeStruct((columns * 16, 128), F32),
            jax.ShapeDtypeStruct((columns, columns), F32),
        ],
        in_specs=[vmem, anywhere, anywhere],
        out_specs=[anywhere, vmem],
        scratch_shapes=[
            pltpu.VMEM((columns, 2 * columns), F32),
            pltpu.VMEM((columns, columns), F32),
            pltpu.VMEM((columns, local), BF16),
            pltpu.VMEM((2, 16, local), BF16),
            pltpu.VMEM((columns * 16, 128), F32),
            pltpu.SemaphoreType.DMA((6,)),
        ],
        compiler_params=pltpu.CompilerParams(vmem_limit_bytes=32 << 20),
        name="finish",
    )(gram, snap, fine)
    return modes.reshape(columns, count_x, count_y, count_z), factor


def solution(mesh):
    return jax.shard_map(
        shards,
        mesh=mesh,
        in_specs=(
            P(None, "sect", "blk", None),
            P(None, "sect", "blk", None),
            P("sect", "blk"),
            P(),
            P(),
        ),
        out_specs=(P(None, "sect", "blk", None), P()),
        check_vma=False,
    )
```

time: 429 us -> 68.8 us (0.16)
  waiting for transfers between devices: 304 us -> 0 us
  Pallas kernels: 0 us -> 63.9 us
  other arithmetic: 58.1 us -> 0 us
  starting transfers between devices: 31.3 us -> 0 us
  between operations: 16.3 us -> 1.3 us
  matrix products: 7.97 us -> 0 us
  local copies, waits for them, and re-layouts: 9.9 us -> 3.32 us
    psum x1 -> x0, waiting for transfers between devices: 300 us -> none  [shards(): gram_total = lax.psum(gram_local, ('sect', 'blk'))]
    pallas_call x0 -> x2, Pallas kernels: none -> 63.9 us  [the longest x1 52.6 us: shards(): pl.pallas_call(functools.partial(gather_kernel, edges), out_shape=[jax.Sh...]
    another operation x8 -> x0, other arithmetic: 53.8 us -> none  [the longest x6 34.1 us: shards(): upper_tri = jnp.linalg.cholesky(gram_total).T]
    ppermute x8 -> x0, starting transfers between devices: 31.3 us -> none  [the longest x4 16.8 us: extended_2(): lax.ppermute(head, axis, [((i + 1) % count, i) for i in range(ends)])]
    dot_general x3 -> x0, matrix products: 4.77 us -> none  [the longest x1 3.62 us: shards(): gram_local = jnp.dot(snapshot, snapshot.T, precision=lax.Precision.HIGHEST)]
    another operation x14 -> x0, local copies, waits for them, and re-layouts: 4.71 us -> none
    ppermute x8 -> x0, waiting for transfers between devices: 4.57 us -> none  [the longest x4 3.98 us: extended_2(): lax.ppermute(head, axis, [((i + 1) % count, i) for i in range(ends)])]
  transfers between devices with their start and end apart: 9 -> 0, of which waited for: 3 -> 0; matrix products, arithmetic and copies ran while one was open for 1% -> 0% of each run, Pallas kernels for 0% -> 0%
where the time goes in v1:
time: 68.8 us; the launch traced here: 68.5 us
  Pallas kernels  63.9 us (93%)
  local copies, waits for them, and re-layouts  3.32 us (5%)
  between operations  1.3 us (2%)
    pallas_call x1, Pallas kernels, shards(): pl.pallas_call(functools.partial(gather_kernel, edges), out_shape=[jax.Sh...  52.6 us
    pallas_call x1, Pallas kernels, shards(): pl.pallas_call(functools.partial(finish_kernel, local * edges[0] * edges[...  11.2 us
    unnamed x8, local copies, waits for them, and re-layouts  3.32 us

profile of v1, /device:TPU:1, one launch (start us, length us, event | category | flops | bytes accessed | tf_op | source)
XLA Modules:
  0.0 68.5 jit_solution(2830707614514878855)
XLA Ops:
  1.3 0.0 copy-start
  1.3 1.2 %copy-done = bf16[246,2,8,128]{3,2,1,0:T(8,128)(2,1)S(1)} copy-done((bf16[246,2,8,128]{3,2,1,0:T(8,128)(2,1)S(1)}, bf16[246,2,8,128]{3,2,1,0:T(8,128)(2,1)}, u32[]{:S(2)}) %copy-start) | copy-done | bytes 1007640
  2.5 0.0 copy-start.1
  2.5 0.8 %copy-done.1 = f32[5,2,8,128]{3,2,1,0:T(8,128)S(1)} copy-done((f32[5,2,8,128]{3,2,1,0:T(8,128)S(1)}, f32[5,2,8,128]{3,2,1,0:T(8,128)}, u32[]{:S(2)}) %copy-start.1) | copy-done | bytes 40984
  3.3 0.0 copy-start.2
  3.3 0.7 %copy-done.2 = f32[5,5]{1,0:T(8,128)S(1)} copy-done((f32[5,5]{1,0:T(8,128)S(1)}, f32[5,5]{1,0:T(8,128)}, u32[]{:S(2)}) %copy-start.2) | copy-done | bytes 124
  4.0 0.0 copy-start.3
  4.0 0.7 copy-done.3
  4.6 52.6 %gather.1 = (f32[256,256]{1,0:T(8,128)S(1)}, bf16[256,2048]{1,0:T(8,128)(2,1)S(1)}, bf16[2,16,2048]{2,1,0:T(8,128)(2,1)S(1)}) custom-call(bf16[246,2,8,128]{3,2,1,0:T(8,128)(2,1)S(1)} %copy-done, f32[5,2,8,128]{3,2,1,0:T(8,128)S(1)} %copy-done.1, s32[1,1]{1,0:T(1,128)S(6)} %copy.7.levels_ref, f32[5]{0:T(128)S(1)} %copy-done.3, f32[5,5]{1,0:T(8,128)S(1)} %copy-done.2), custom_call_target="tpu_custom_call" | custom-call | tf_op jit(solution)/shard_map/gather/pallas_call | solution.py:410
  57.2 11.2 %finish.1 = (f32[4096,128]{1,0:T(8,128)}, f32[256,256]{1,0:T(8,128)}) custom-call(f32[256,256]{1,0:T(8,128)S(1)} %get-tuple-element.7.gram_ref, bf16[256,2048]{1,0:T(8,128)(2,1)S(1)} %get-tuple-element.8.snap_ref, bf16[2,16,2048]{2,1,0:T(8,128)(2,1)S(1)} %get-tuple-element.9.fine_ref), custom_call_target="tpu_custom_call" | custom-call | tf_op jit(solution)/shard_map/finish/pallas_call | solution.py:447
Async XLA Ops:
  1.3 1.2 %copy-start = (bf16[246,2,8,128]{3,2,1,0:T(8,128)(2,1)S(1)}, bf16[246,2,8,128]{3,2,1,0:T(8,128)(2,1)}, u32[]{:S(2)}) copy-start(bf16[246,2,8,128]{3,2,1,0:T(8,128)(2,1)} %hist_ref.1) | copy-start | bytes 3022852
  2.5 0.8 %copy-start.1 = (f32[5,2,8,128]{3,2,1,0:T(8,128)S(1)}, f32[5,2,8,128]{3,2,1,0:T(8,128)}, u32[]{:S(2)}) copy-start(f32[5,2,8,128]{3,2,1,0:T(8,128)} %fields_ref.1) | copy-start | bytes 122884
  3.3 0.7 %copy-start.2 = (f32[5,5]{1,0:T(8,128)S(1)}, f32[5,5]{1,0:T(8,128)}, u32[]{:S(2)}) copy-start(f32[5,5]{1,0:T(8,128)} %coup_ref.1) | copy-start | bytes 304
  4.0 0.7 copy-start.3

commit v2 on v0

v2 whole, which is shorter than its diff:
```python
import functools
import math

import jax
import jax.numpy as jnp
from jax import lax
from jax.experimental import pallas as pl
from jax.experimental.pallas import tpu as pltpu
from jax.sharding import PartitionSpec as P

F32 = jnp.float32
BF16 = jnp.bfloat16
MESH = pl.DeviceIdType.MESH
Z_CHIPS = 8
Y_CHIPS = 8
X_LOW = 4
RING = 8
BLOCK = 32
GROUP = 16
HALF = 128
TAIL = 16


def position():
    sect = lax.axis_index("sect")
    blk = lax.axis_index("blk")
    x = (sect // Z_CHIPS) * X_LOW + blk // (2 * Y_CHIPS)
    y = (blk // 2) % Y_CHIPS
    return x, y, sect % Z_CHIPS, blk % 2


def device(x, y, z, core):
    return ((x // X_LOW) * Z_CHIPS + z, ((x % X_LOW) * Y_CHIPS + y) * 2 + core)


def neighbour_sum(cells, sect_low, sect_high, blk_low, blk_high, sub, lane):
    out = []
    for f in range(len(cells)):
        row = []
        for x in range(2):
            c = cells[f][x]
            low = sect_low[f] if x == 0 else cells[f][0]
            high = sect_high[f] if x == 1 else cells[f][1]
            up = jnp.where(sub == 0, jnp.broadcast_to(blk_low[2 * f + x], (8, 128)), pltpu.roll(c, 1, 0))
            down = jnp.where(sub == 7, jnp.broadcast_to(blk_high[2 * f + x], (8, 128)), pltpu.roll(c, 7, 0))
            left = jnp.where(lane == 0, 0.0, pltpu.roll(c, 1, 1))
            right = jnp.where(lane == 127, 0.0, pltpu.roll(c, 127, 1))
            row.append(((high + low) + (down + up) + (right + left)) - 6.0 * c)
        out.append(row)
    return out


def tendency(cells, beside, diffusivity, coupling):
    count = len(cells)
    out = []
    for f in range(count):
        row = []
        for x in range(2):
            total = coupling[f, 0] * cells[0][x]
            for g in range(1, count):
                total = total + coupling[f, g] * cells[g][x]
            row.append(diffusivity[f] * beside[f][x] + total)
        out.append(row)
    return out


def split3(x):
    high = x.astype(BF16)
    rest = x - high.astype(F32)
    mid = rest.astype(BF16)
    low = (rest - mid.astype(F32)).astype(BF16)
    return high, mid, low


def dot_rows(a, b):
    return lax.dot_general(a, b, (((1,), (1,)), ((), ())), preferred_element_type=F32)


def dot_columns(a, b):
    return lax.dot_general(a, b, (((0,), (0,)), ((), ())), preferred_element_type=F32)


def eliminate(rows, col0):
    size, width = rows.shape
    count = size // 8
    tiles = width // 128
    values = [rows[8 * v:8 * v + 8] for v in range(count)]
    pivots = [jnp.zeros((8, 128), F32) for _ in range(count)]
    sub = lax.broadcasted_iota(jnp.int32, (8, 128), 0)
    for start in range(0, size, GROUP):
        v0 = start // 8
        spread = [
            [jnp.broadcast_to(values[v][:, col0 + start + p:col0 + start + p + 1], (8, 128)) for v in range(v0, count)]
            for p in range(GROUP)
        ]
        for p in range(GROUP):
            vp, s = (start + p) // 8, (start + p) % 8
            raw = spread[p]
            pivot = jnp.broadcast_to(raw[vp - v0][s:s + 1, :], (8, 128))
            inverse = 1.0 / pivot
            pivots[vp] = jnp.where(sub == s, pivot, pivots[vp])
            factors = {}
            for v in range(vp, count):
                factor = raw[v - v0] * inverse
                factors[v] = jnp.where(sub > s, factor, 0.0) if v == vp else factor
            for later in range(p + 1, GROUP):
                vl, sl = (start + later) // 8, (start + later) % 8
                across = jnp.broadcast_to(raw[vl - v0][sl:sl + 1, :], (8, 128))
                for v in range(vp, count):
                    spread[later][v - v0] = spread[later][v - v0] - factors[v] * across
            row = jnp.broadcast_to(values[vp][s:s + 1, :], (8, width))
            for v in range(vp, count):
                if v == vp and s == 7:
                    continue
                values[v] = values[v] - jnp.concatenate([factors[v]] * tiles, axis=1) * row
    return jnp.concatenate(
        [values[v] * jnp.concatenate([lax.rsqrt(pivots[v])] * tiles, axis=1) for v in range(count)], axis=0
    )


def pack_left(x, axis):
    h, m, l = split3(x)
    return jnp.concatenate([h, h, m, m, h, l], axis=axis)


def pack_right(x, axis):
    h, m, l = split3(x)
    return jnp.concatenate([h, m, h, m, l, h], axis=axis)


def eliminate_half(work, ends, store, between):
    b0 = 0
    rows = work[0:ends[0], :]
    for index, b1 in enumerate(ends):
        done = eliminate(rows, b0)
        i = lax.broadcasted_iota(jnp.int32, (b1 - b0, HALF), 0) + b0
        j = lax.broadcasted_iota(jnp.int32, (b1 - b0, HALF), 1)
        upper = jnp.where(j >= i, done[:, :HALF], 0.0)
        store(b0, b1, upper, done[:, HALF:])
        if index + 1 < len(ends):
            b2 = ends[index + 1]
            left = pack_left(upper, 0)
            right = pack_right(done, 0)
            rows = work[b1:b2, :] - dot_columns(left[:, b1:b2], right)
            if index + 2 < len(ends):
                b3 = ends[-1]
                work[b2:b3, :] = work[b2:b3, :] - dot_columns(left[:, b2:b3], right)
        between(index)
        b0 = b1


def gather_kernel(
    edges, total_rows,
    hist_ref, fields_ref, levels_ref, diff_ref, coup_ref,
    inverse_ref, upper_ref, snap, fine,
    hist, wide, fields, diff, coup,
    edge_sect, edge_blk, stage_blk, stage_sect,
    p_send, p_half, p_slots, p_part, p_final,
    h_send, h_half, h_slots, h_part, h_final,
    f_send, f_half, f_slots, f_part, f_final,
    work, work2,
    local_sem, send_sem, recv_sem,
):
    n_sect, n_blk = edges
    sect = lax.axis_index("sect")
    blk = lax.axis_index("blk")
    x, y, z, core = position()
    other = device(x, y, z, 1 - core)
    along_x = [device((x + k) % RING, y, z, core) for k in range(1, RING)]
    along_y = [device(x, (y + k) % RING, z, core) for k in range(1, RING)]
    along_z = [device(x, y, (z + k) % RING, core) for k in range(1, RING)]
    along = [along_x, along_y, along_z]
    sect_down = ((sect + n_sect - 1) % n_sect, blk)
    sect_up = ((sect + 1) % n_sect, blk)
    blk_down = (sect, (blk + n_blk - 1) % n_blk)
    blk_up = (sect, (blk + 1) % n_blk)
    peers = [other] + along_x + along_y + along_z + [sect_down, sect_up, blk_down, blk_up]

    count = fields_ref.shape[0]
    stored = hist_ref.shape[0]
    columns = stored + 2 * count
    scale = math.sqrt(total_rows)

    loads = [
        pltpu.make_async_copy(hist_ref.at[0:HALF], hist.at[0:HALF], local_sem.at[0]),
        pltpu.make_async_copy(fields_ref, fields, local_sem.at[1]),
        pltpu.make_async_copy(hist_ref.at[HALF:stored], hist.at[HALF:stored], local_sem.at[2]),
        pltpu.make_async_copy(diff_ref, diff, local_sem.at[3]),
        pltpu.make_async_copy(coup_ref, coup, local_sem.at[4]),
    ]
    for load in loads:
        load.start()
    barrier = pltpu.get_barrier_semaphore()
    for peer in peers:
        pl.semaphore_signal(barrier, inc=1, device_id=peer, device_id_type=MESH)

    def send(src, dst, index, target):
        pltpu.make_async_remote_copy(
            src_ref=src, dst_ref=dst, send_sem=send_sem.at[index], recv_sem=recv_sem.at[index],
            device_id=target, device_id_type=MESH,
        ).start()

    def wait_recv(ref, index):
        pltpu.make_async_copy(ref, ref, recv_sem.at[index]).wait()

    def wait_send(ref, index):
        pltpu.make_async_copy(ref, ref, send_sem.at[index]).wait()

    sub = lax.broadcasted_iota(jnp.int32, (8, 128), 0)
    lane = lax.broadcasted_iota(jnp.int32, (8, 128), 1)

    wide[stored * 16:, :] = jnp.zeros((2 * count * 16, 128), F32)
    loads[1].wait()
    cells = [[fields[f, k] for k in range(2)] for f in range(count)]

    def send_edges(values, first):
        for f in range(count):
            for k in range(2):
                stage_sect[first, k, f] = values[f][k]
                stage_blk[first, 0, 2 * f + k:2 * f + k + 1, :] = values[f][k][0:1, :]
                stage_blk[first, 1, 2 * f + k:2 * f + k + 1, :] = values[f][k][7:8, :]
        send(stage_sect.at[first, 0], edge_sect.at[first, 1], 2 * first, sect_down)
        send(stage_sect.at[first, 1], edge_sect.at[first, 0], 2 * first, sect_up)
        send(stage_blk.at[first, 0], edge_blk.at[first, 1], 2 * first + 1, blk_down)
        send(stage_blk.at[first, 1], edge_blk.at[first, 0], 2 * first + 1, blk_up)

    def take_edges(first):
        wait_recv(edge_sect.at[first], 2 * first)
        wait_recv(edge_blk.at[first], 2 * first + 1)
        sect_low = [jnp.where(sect == 0, 0.0, edge_sect[first, 0, f]) for f in range(count)]
        sect_high = [jnp.where(sect == n_sect - 1, 0.0, edge_sect[first, 1, f]) for f in range(count)]
        blk_low = [jnp.where(blk == 0, 0.0, edge_blk[first, 0, r:r + 1, :]) for r in range(2 * count)]
        blk_high = [jnp.where(blk == n_blk - 1, 0.0, edge_blk[first, 1, r:r + 1, :]) for r in range(2 * count)]
        return sect_low, sect_high, blk_low, blk_high

    pl.semaphore_wait(barrier, len(peers))
    send_edges(cells, 0)

    def arrange(low, high, full):
        wide[low * 16:high * 16, :] = hist[low:high].astype(F32).reshape((high - low) * 16, 128)
        for q in range(16):
            snap[low:full, 128 * q:128 * q + 128] = wide[pl.ds(low * 16 + q, full - low, stride=16), :].astype(BF16)

    loads[0].wait()
    arrange(0, HALF, HALF)
    first = snap[0:HALF, :]
    square = dot_rows(first, first)
    third = HALF // 8
    for part in range(3):
        p_send[0, part] = square[third * part:third * part + third, :]
    p_send[1, 0] = square[3 * third:4 * third, :]
    corner = jnp.concatenate([square[64:96, 64:], square[96:128, 64:]], axis=1)
    p_send[1, 1] = corner[0:16]
    p_send[1, 2] = corner[16:32]
    send(p_send.at[1 - core], p_half, 4, other)

    loads[2].wait()
    arrange(HALF, stored, columns)
    second = snap[HALF:columns, :]
    h_send[0] = dot_rows(first, second).reshape(RING, 16, 128)
    h_send[1] = dot_rows(second, second).reshape(RING, 16, 128)
    send(h_send.at[1 - core], h_half.at[0], 5, other)

    def p_phase(phase):
        for k in range(RING - 1):
            for part in range(3):
                send(p_part.at[phase, part], p_slots.at[phase, part, k], 6 + phase, along[(part + phase) % 3][k])

    def p_sum(phase):
        wait_recv(p_slots.at[phase], 6 + phase)
        total = p_part[phase]
        for k in range(RING - 1):
            total = total + p_slots[phase, :, k]
        return total

    def total_of(own, slots):
        for k in range(RING - 1):
            own = own + slots[k]
        return own

    wait_recv(p_half, 4)
    p_part[0] = p_send[core] + p_half[...]
    p_phase(0)

    wait_recv(h_half.at[0], 5)
    h_half[1] = h_send[core] + h_half[0]
    for k in range(1, RING):
        send(h_half.at[1, (y + k) % RING], h_slots.at[0, k - 1], 9, along_y[k - 1])

    for load in loads[3:]:
        load.wait()
    refined = (jnp.zeros((8, 128), jnp.int32) + levels_ref[0, 0]).astype(F32)
    stride = 1.0 / (1.0 + refined)
    diffusivity = [jnp.broadcast_to(diff[0:1, f:f + 1], (8, 128)) for f in range(count)]
    coupling = {
        (f, g): jnp.broadcast_to(coup[f:f + 1, g:g + 1], (8, 128)) for f in range(count) for g in range(count)
    }
    beside = neighbour_sum(cells, *take_edges(0), sub, lane)
    tend = tendency(cells, beside, diffusivity, coupling)
    first_state = [[cells[f][k] + stride * tend[f][k] for k in range(2)] for f in range(count)]
    send_edges(first_state, 1)

    p_part[1] = p_sum(0)
    p_phase(1)

    wait_recv(h_slots.at[0], 9)
    h_part[0] = total_of(h_half[1, y], h_slots[0])
    for k in range(1, RING):
        send(h_part.at[0], h_slots.at[1, k - 1], 10, along_x[k - 1])

    p_part[2] = p_sum(1)
    p_phase(2)

    wait_recv(h_slots.at[1], 10)
    h_part[1] = total_of(h_part[0], h_slots[1])
    for k in range(1, RING):
        send(h_part.at[1], h_slots.at[2, k - 1], 11, along_z[k - 1])

    beside = neighbour_sum(first_state, *take_edges(1), sub, lane)
    tend = tendency(first_state, beside, diffusivity, coupling)
    weight = refined * stride
    for f in range(count):
        for k in range(2):
            final = first_state[f][k] + weight * tend[f][k]
            row = (stored + f) * 16 + 8 * k
            wide[row:row + 8, :] = final
            row = (stored + count + f) * 16 + 8 * k
            wide[row:row + 8, :] = final - cells[f][k]
    for q in range(16):
        high, mid, low = split3(wide[pl.ds((columns - TAIL) * 16 + q, TAIL, stride=16), :])
        snap[columns - TAIL:columns, 128 * q:128 * q + 128] = high
        fine[0, :, 128 * q:128 * q + 128] = mid
        fine[1, :, 128 * q:128 * q + 128] = low
    pieces = jnp.concatenate([snap[columns - TAIL:columns, :], fine[0], fine[1]], axis=0)
    fresh = dot_rows(pieces, snap[...])
    fresh_fine = dot_rows(pieces, pieces[TAIL:])
    fresh = fresh[0:TAIL] + fresh[TAIL:2 * TAIL] + fresh[2 * TAIL:]
    extra = fresh_fine[0:TAIL, 0:TAIL] + (fresh_fine[0:TAIL, TAIL:] + fresh_fine[TAIL:2 * TAIL, 0:TAIL])
    f_send[0] = fresh[:, :HALF]
    f_send[1] = fresh[:, HALF:]
    f_send[1, :, HALF - TAIL:] = fresh[:, columns - TAIL:] + extra
    send(f_send.at[1 - core], f_half.at[0], 12, other)

    wait_recv(f_half.at[0], 12)
    f_part[0] = f_send[core] + f_half[0]
    for k in range(1, RING):
        send(f_part.at[0], f_slots.at[0, k - 1], 13, along_x[k - 1])

    p_final[core] = p_sum(2)
    send(p_final.at[core], p_final.at[core], 14, other)

    wait_recv(h_slots.at[2], 11)
    h_final[core, y] = total_of(h_part[1], h_slots[2])
    for k in range(1, RING):
        send(h_final.at[core, y], h_final.at[core, y], 15, along_y[k - 1])

    wait_recv(p_final.at[0], 14)

    i = lax.broadcasted_iota(jnp.int32, (HALF, HALF), 0)
    j = lax.broadcasted_iota(jnp.int32, (HALF, HALF), 1)
    identity = (i == j).astype(F32)
    for part in range(3):
        work[16 * part:16 * part + 16, 0:HALF] = p_final[0, part]
    work[48:64, 0:HALF] = p_final[1, 0]
    lower = jnp.concatenate([p_final[1, 1], p_final[1, 2]], axis=0)
    work[64:96, 0:HALF] = jnp.concatenate([jnp.zeros((32, 64), F32), lower[:, :64]], axis=1)
    work[96:128, 0:HALF] = jnp.concatenate([jnp.zeros((32, 64), F32), lower[:, 64:]], axis=1)
    work[:, HALF:] = identity
    inverse_ref[0:HALF, HALF:] = jnp.zeros((HALF, HALF), F32)
    inverse_ref[columns - TAIL:, :] = jnp.zeros((TAIL, columns), F32)
    upper_ref[HALF:, 0:HALF] = jnp.zeros((HALF, HALF), F32)

    def store_first(b0, b1, upper, solved):
        upper_ref[b0:b1, 0:HALF] = upper * (1.0 / scale)
        inverse_ref[b0:b1, 0:HALF] = solved

    def between_first(index):
        if index == 1:
            wait_recv(f_slots.at[0], 13)
            f_part[1] = total_of(f_part[0], f_slots[0])
            for k in range(1, RING):
                send(f_part.at[1], f_slots.at[1, k - 1], 16, along_z[k - 1])

    eliminate_half(work, [32, 64, 96, 128], store_first, between_first)

    wait_recv(h_slots.at[2], 15)
    send(h_final.at[core], h_final.at[core], 17, other)
    wait_recv(f_slots.at[1], 16)
    f_part[2] = total_of(f_part[1], f_slots[1])
    for k in range(1, RING):
        send(f_part.at[2], f_slots.at[2, k - 1], 18, along_y[k - 1])
    wait_recv(h_final.at[0], 17)

    solved = inverse_ref[0:HALF, 0:HALF]
    side = jnp.dot(
        pack_left(solved, 1), pack_right(h_final[0].reshape(HALF, HALF), 0), preferred_element_type=F32
    )
    product = dot_columns(pack_left(side, 0), pack_right(jnp.concatenate([side, solved], axis=1), 0))
    work2[:, 0:HALF] = h_final[1].reshape(HALF, HALF) - product[:, :HALF]
    work2[:, HALF:2 * HALF] = -product[:, HALF:]
    work2[:, 2 * HALF:] = identity
    upper_ref[0:HALF, HALF:] = side * (1.0 / scale)

    def store_second(b0, b1, upper, solved):
        upper_ref[HALF + b0:HALF + b1, HALF:] = upper * (1.0 / scale)
        inverse_ref[HALF + b0:HALF + b1, :] = solved

    def between_second(index):
        if index == 2:
            wait_recv(f_slots.at[2], 18)
            f_final[core] = total_of(f_part[2], f_slots[2])
            send(f_final.at[core], f_final.at[core], 19, other)

    eliminate_half(work2, [32, 64, 96, HALF - TAIL], store_second, between_second)

    wait_recv(f_final.at[0], 19)
    row = lax.broadcasted_iota(jnp.int32, (TAIL, columns), 0)
    col = lax.broadcasted_iota(jnp.int32, (TAIL, columns), 1)
    last = jnp.concatenate([f_final[0], f_final[1]], axis=1)
    solved = inverse_ref[...]
    below = dot_rows(
        pack_left(jnp.where(col < columns - TAIL, last, 0.0), 1), pack_right(solved, 1)
    )
    left = pack_left(below, 1)
    placed = jnp.concatenate([jnp.zeros((HALF - TAIL, columns), F32), below], axis=0)
    rest = last[:, HALF:] - dot_rows(left, pack_right(placed, 1))
    onward = (col == row + (columns - TAIL)).astype(F32) - jnp.dot(
        left, pack_right(solved, 0), preferred_element_type=F32
    )
    done = eliminate(jnp.concatenate([rest, onward], axis=1), HALF - TAIL)
    inverse_ref[columns - TAIL:, :] = done[:, HALF:]
    turned = placed.T
    right_lanes = lax.broadcasted_iota(jnp.int32, (columns - TAIL, HALF), 1) >= HALF - TAIL
    upper_ref[0:columns - TAIL, HALF:] = jnp.where(
        right_lanes, turned[0:columns - TAIL] * (1.0 / scale), upper_ref[0:columns - TAIL, HALF:]
    )
    row = lax.broadcasted_iota(jnp.int32, (TAIL, HALF), 0)
    col = lax.broadcasted_iota(jnp.int32, (TAIL, HALF), 1)
    upper_ref[columns - TAIL:, HALF:] = jnp.where(
        col >= row + (HALF - TAIL), done[:, :HALF] * (1.0 / scale), 0.0
    )

    for round_ in range(2):
        wait_send(edge_sect.at[round_], 2 * round_)
        wait_send(edge_blk.at[round_], 2 * round_ + 1)
    wait_send(p_half, 4)
    wait_send(h_half.at[0], 5)
    for phase in range(3):
        wait_send(p_slots.at[phase], 6 + phase)
        wait_send(h_slots.at[phase], 9 + phase)
    wait_send(f_half.at[0], 12)
    wait_send(f_slots.at[0], 13)
    wait_send(p_final.at[0], 14)
    wait_send(h_slots.at[0], 15)
    wait_send(f_slots.at[1], 16)
    wait_send(h_final.at[0], 17)
    wait_send(f_slots.at[2], 18)
    wait_send(f_final.at[0], 19)


def finish_kernel(
    total_rows,
    inverse_ref, upper_ref, snap, fine,
    modes_ref, factor_ref,
    modes, local_sem,
):
    size = inverse_ref.shape[0]
    scale = math.sqrt(total_rows)
    keep = pltpu.make_async_copy(upper_ref, factor_ref, local_sem.at[0])
    keep.start()
    step = 64
    stores = []
    tail = jnp.concatenate([fine[0], fine[0], fine[0], fine[1]], axis=0)
    for r0 in range(0, size, step):
        h, m, l = split3(inverse_ref[r0:r0 + step, :] * scale)
        out = jnp.dot(h, snap[...], preferred_element_type=F32)
        out = out + jnp.dot(m, snap[...], preferred_element_type=F32)
        out = out + jnp.dot(l, snap[...], preferred_element_type=F32)
        last = jnp.concatenate(
            [h[:, size - TAIL:], m[:, size - TAIL:], l[:, size - TAIL:], h[:, size - TAIL:]], axis=1
        )
        out = out + jnp.dot(last, tail, preferred_element_type=F32)
        for q in range(16):
            modes[pl.ds(r0 * 16 + q, step, stride=16), :] = out[:, 128 * q:128 * q + 128]
        store = pltpu.make_async_copy(
            modes.at[pl.ds(r0 * 16, step * 16)], modes_ref.at[pl.ds(r0 * 16, step * 16)], local_sem.at[1 + r0 // step]
        )
        store.start()
        stores.append(store)
    keep.wait()
    for store in stores:
        store.wait()


def in_hbm(array):
    return pltpu.with_memory_space_constraint(array, pltpu.HBM)


def shards(fields, history, levels, diffusivity, coupling):
    edges = (lax.axis_size("sect"), lax.axis_size("blk"))
    stored, count_x, count_y, count_z = history.shape
    count = fields.shape[0]
    columns = stored + 2 * count
    local = count_x * count_y * count_z
    total_rows = local * edges[0] * edges[1]
    vmem = pl.BlockSpec(memory_space=pltpu.VMEM)
    hbm = pl.BlockSpec(memory_space=pltpu.HBM)
    smem = pl.BlockSpec(memory_space=pltpu.SMEM)
    tile = (16, 128)
    inverse, upper, snap, fine = pl.pallas_call(
        functools.partial(gather_kernel, edges, total_rows),
        out_shape=[
            jax.ShapeDtypeStruct((columns, columns), F32),
            jax.ShapeDtypeStruct((columns, columns), F32),
            jax.ShapeDtypeStruct((columns, local), BF16),
            jax.ShapeDtypeStruct((2, TAIL, local), BF16),
        ],
        in_specs=[hbm, hbm, smem, hbm, hbm],
        out_specs=[vmem, vmem, vmem, vmem],
        scratch_shapes=[
            pltpu.VMEM(history.shape, BF16),
            pltpu.VMEM((columns * 16, 128), F32),
            pltpu.VMEM(fields.shape, F32),
            pltpu.VMEM((1, count), F32),
            pltpu.VMEM((count, count), F32),
            pltpu.VMEM((2, 2, count, 8, 128), F32),
            pltpu.VMEM((2, 2, 16, 128), F32),
            pltpu.VMEM((2, 2, 16, 128), F32),
            pltpu.VMEM((2, 2, count, 8, 128), F32),
            pltpu.VMEM((2, 3) + tile, F32),
            pltpu.VMEM((3,) + tile, F32),
            pltpu.VMEM((3, 3, RING - 1) + tile, F32),
            pltpu.VMEM((3, 3) + tile, F32),
            pltpu.VMEM((2, 3) + tile, F32),
            pltpu.VMEM((2, RING) + tile, F32),
            pltpu.VMEM((2, RING) + tile, F32),
            pltpu.VMEM((3, RING - 1) + tile, F32),
            pltpu.VMEM((2,) + tile, F32),
            pltpu.VMEM((2, RING) + tile, F32),
            pltpu.VMEM((2,) + tile, F32),
            pltpu.VMEM((1,) + tile, F32),
            pltpu.VMEM((3, RING - 1) + tile, F32),
            pltpu.VMEM((3,) + tile, F32),
            pltpu.VMEM((2,) + tile, F32),
            pltpu.VMEM((HALF, 2 * HALF), F32),
            pltpu.VMEM((HALF, 3 * HALF), F32),
            pltpu.SemaphoreType.DMA((5,)),
            pltpu.SemaphoreType.DMA((20,)),
            pltpu.SemaphoreType.DMA((20,)),
        ],
        compiler_params=pltpu.CompilerParams(
            collective_id=0, has_side_effects=True, vmem_limit_bytes=32 << 20
        ),
        name="gather",
    )(in_hbm(history), in_hbm(fields), levels, in_hbm(diffusivity.reshape(1, count)), in_hbm(coupling))
    modes, factor = pl.pallas_call(
        functools.partial(finish_kernel, total_rows),
        out_shape=[
            jax.ShapeDtypeStruct((columns * 16, 128), F32),
            jax.ShapeDtypeStruct((columns, columns), F32),
        ],
        in_specs=[vmem, vmem, vmem, vmem],
        out_specs=[hbm, hbm],
        scratch_shapes=[
            pltpu.VMEM((columns * 16, 128), F32),
            pltpu.SemaphoreType.DMA((5,)),
        ],
        compiler_params=pltpu.CompilerParams(vmem_limit_bytes=32 << 20),
        name="finish",
    )(inverse, upper, snap, fine)
    return modes.reshape(columns, count_x, count_y, count_z), factor


def solution(mesh):
    return jax.shard_map(
        shards,
        mesh=mesh,
        in_specs=(
            P(None, "sect", "blk", None),
            P(None, "sect", "blk", None),
            P("sect", "blk"),
            P(),
            P(),
        ),
        out_specs=(P(None, "sect", "blk", None), P()),
        check_vma=False,
    )
```

time: 429 us -> 64.4 us (0.15)
  waiting for transfers between devices: 304 us -> 0 us
  Pallas kernels: 0 us -> 62.9 us
  other arithmetic: 58.1 us -> 0 us
  starting transfers between devices: 31.3 us -> 0 us
  between operations: 16.3 us -> 1.28 us
  local copies, waits for them, and re-layouts: 9.9 us -> 0 us
  matrix products: 7.97 us -> 0 us
    psum x1 -> x0, waiting for transfers between devices: 300 us -> none  [shards(): gram_total = lax.psum(gram_local, ('sect', 'blk'))]
    pallas_call x0 -> x2, Pallas kernels: none -> 62.9 us  [the longest x1 59.1 us: shards(): pl.pallas_call(functools.partial(gather_kernel, edges, total_rows), out_s...]
    another operation x8 -> x0, other arithmetic: 53.8 us -> none  [the longest x6 34.1 us: shards(): upper_tri = jnp.linalg.cholesky(gram_total).T]
    ppermute x8 -> x0, starting transfers between devices: 31.3 us -> none  [the longest x4 16.8 us: extended_2(): lax.ppermute(head, axis, [((i + 1) % count, i) for i in range(ends)])]
    dot_general x3 -> x0, matrix products: 4.77 us -> none  [the longest x1 3.62 us: shards(): gram_local = jnp.dot(snapshot, snapshot.T, precision=lax.Precision.HIGHEST)]
    another operation x14 -> x0, local copies, waits for them, and re-layouts: 4.71 us -> none
    ppermute x8 -> x0, waiting for transfers between devices: 4.57 us -> none  [the longest x4 3.98 us: extended_2(): lax.ppermute(head, axis, [((i + 1) % count, i) for i in range(ends)])]
  transfers between devices with their start and end apart: 9 -> 0, of which waited for: 3 -> 0; matrix products, arithmetic and copies ran while one was open for 1% -> 0% of each run, Pallas kernels for 0% -> 0%
where the time goes in v2:
time: 64.4 us; the launch traced here: 64.2 us
  Pallas kernels  62.9 us (98%)
  between operations  1.28 us (2%)
    pallas_call x1, Pallas kernels, shards(): pl.pallas_call(functools.partial(gather_kernel, edges, total_rows), out_s...  59.1 us
    pallas_call x1, Pallas kernels, shards(): pl.pallas_call(functools.partial(finish_kernel, total_rows), out_shape=[j...  3.83 us

profile of v2, /device:TPU:1, one launch (start us, length us, event | category | flops | bytes accessed | tf_op | source)
XLA Modules:
  0.0 64.2 jit_solution(5538700759826699614)
XLA Ops:
  1.3 59.1 %gather.1 = (f32[256,256]{1,0:T(8,128)S(1)}, f32[256,256]{1,0:T(8,128)S(1)}, bf16[256,2048]{1,0:T(8,128)(2,1)S(1)}, bf16[2,16,2048]{2,1,0:T(8,128)(2,1)S(1)}) custom-call(bf16[246,2,8,128]{3,2,1,0:T(8,128)(2,1)} %hist_ref.1, f32[5,2,8,128]{3,2,1,0:T(8,128)} %fields_ref.1, s32[1,1]{1,0:T(1,128)S(6)} %copy.7.levels_ref, f32[1,5]{1,0:T(1,128)} %bitcast.2, ...), custom_call_target="tpu_custom_call" | custom-call | tf_op jit(solution)/shard_map/gather/pallas_call | solution.py:510
  60.4 3.8 %finish.1 = (f32[4096,128]{1,0:T(8,128)}, f32[256,256]{1,0:T(8,128)}) custom-call(f32[256,256]{1,0:T(8,128)S(1)} %get-tuple-element.8.inverse_ref, f32[256,256]{1,0:T(8,128)S(1)} %get-tuple-element.9.upper_ref, bf16[256,2048]{1,0:T(8,128)(2,1)S(1)} %get-tuple-element.10.snap, bf16[2,16,2048]{2,1,0:T(8,128)(2,1)S(1)} %get-tuple-element.11.fine), custom_call_target="tpu_custom_call" | custom-call | tf_op jit(solution)/shard_map/finish/pallas_call | solution.py:556

commit v3 on v2

--- a/solution.py
+++ b/solution.py
@@ -33,34 +33,25 @@
     return ((x // X_LOW) * Z_CHIPS + z, ((x % X_LOW) * Y_CHIPS + y) * 2 + core)
 
 
-def neighbour_sum(cells, sect_low, sect_high, blk_low, blk_high, sub, lane):
+def along_z(cells, lane):
+    left = jnp.where(lane == 0, 0.0, pltpu.roll(cells, 1, 1))
+    right = jnp.where(lane == 127, 0.0, pltpu.roll(cells, 127, 1))
+    return right + left
+
+
+def along_y(cells, low_row, high_row, sub):
+    low = jnp.where(sub == 0, jnp.broadcast_to(low_row, (8, 128)), pltpu.roll(cells, 1, 0))
+    high = jnp.where(sub == 7, jnp.broadcast_to(high_row, (8, 128)), pltpu.roll(cells, 7, 0))
+    return high + low
+
+
+def slab_tendency(slab, beside, diffusivity, coupling):
     out = []
-    for f in range(len(cells)):
-        row = []
-        for x in range(2):
-            c = cells[f][x]
-            low = sect_low[f] if x == 0 else cells[f][0]
-            high = sect_high[f] if x == 1 else cells[f][1]
-            up = jnp.where(sub == 0, jnp.broadcast_to(blk_low[2 * f + x], (8, 128)), pltpu.roll(c, 1, 0))
-            down = jnp.where(sub == 7, jnp.broadcast_to(blk_high[2 * f + x], (8, 128)), pltpu.roll(c, 7, 0))
-            left = jnp.where(lane == 0, 0.0, pltpu.roll(c, 1, 1))
-            right = jnp.where(lane == 127, 0.0, pltpu.roll(c, 127, 1))
-            row.append(((high + low) + (down + up) + (right + left)) - 6.0 * c)
-        out.append(row)
-    return out
-
-
-def tendency(cells, beside, diffusivity, coupling):
-    count = len(cells)
-    out = []
-    for f in range(count):
-        row = []
-        for x in range(2):
-            total = coupling[f, 0] * cells[0][x]
-            for g in range(1, count):
-                total = total + coupling[f, g] * cells[g][x]
-            row.append(diffusivity[f] * beside[f][x] + total)
-        out.append(row)
+    for f in range(len(slab)):
+        total = coupling[f, 0] * slab[0]
+        for g in range(1, len(slab)):
+            total = total + coupling[f, g] * slab[g]
+        out.append(diffusivity[f] * (beside[f] - 6.0 * slab[f]) + total)
     return out
 
 
@@ -153,8 +144,8 @@
     edges, total_rows,
     hist_ref, fields_ref, levels_ref, diff_ref, coup_ref,
     inverse_ref, upper_ref, snap, fine,
-    hist, wide, fields, diff, coup,
-    edge_sect, edge_blk, stage_blk, stage_sect,
+    hist, newest, fields, diff, coup,
+    edge_sect, edge_blk, edge_corner, stage_blk, block,
     p_send, p_half, p_slots, p_part, p_final,
     h_send, h_half, h_slots, h_part, h_final,
     f_send, f_half, f_slots, f_part, f_final,
@@ -166,15 +157,16 @@
     blk = lax.axis_index("blk")
     x, y, z, core = position()
     other = device(x, y, z, 1 - core)
-    along_x = [device((x + k) % RING, y, z, core) for k in range(1, RING)]
-    along_y = [device(x, (y + k) % RING, z, core) for k in range(1, RING)]
-    along_z = [device(x, y, (z + k) % RING, core) for k in range(1, RING)]
-    along = [along_x, along_y, along_z]
-    sect_down = ((sect + n_sect - 1) % n_sect, blk)
-    sect_up = ((sect + 1) % n_sect, blk)
-    blk_down = (sect, (blk + n_blk - 1) % n_blk)
-    blk_up = (sect, (blk + 1) % n_blk)
-    peers = [other] + along_x + along_y + along_z + [sect_down, sect_up, blk_down, blk_up]
+    over_x = [device((x + k) % RING, y, z, core) for k in range(1, RING)]
+    over_y = [device(x, (y + k) % RING, z, core) for k in range(1, RING)]
+    over_z = [device(x, y, (z + k) % RING, core) for k in range(1, RING)]
+    over = [over_x, over_y, over_z]
+    sects = [(sect + n_sect - 1) % n_sect, (sect + 1) % n_sect]
+    blks = [(blk + n_blk - 1) % n_blk, (blk + 1) % n_blk]
+    sect_beside = [(s, blk) for s in sects]
+    blk_beside = [(sect, b) for b in blks]
+    corners = [[(s, b) for b in blks] for s in sects]
+    peers = [other] + over_x + over_y + over_z + sect_beside + blk_beside + corners[0] + corners[1]
 
     count = fields_ref.shape[0]
     stored = hist_ref.shape[0]
@@ -209,41 +201,31 @@
     sub = lax.broadcasted_iota(jnp.int32, (8, 128), 0)
     lane = lax.broadcasted_iota(jnp.int32, (8, 128), 1)
 
-    wide[stored * 16:, :] = jnp.zeros((2 * count * 16, 128), F32)
     loads[1].wait()
     cells = [[fields[f, k] for k in range(2)] for f in range(count)]
 
-    def send_edges(values, first):
-        for f in range(count):
-            for k in range(2):
-                stage_sect[first, k, f] = values[f][k]
-                stage_blk[first, 0, 2 * f + k:2 * f + k + 1, :] = values[f][k][0:1, :]
-                stage_blk[first, 1, 2 * f + k:2 * f + k + 1, :] = values[f][k][7:8, :]
-        send(stage_sect.at[first, 0], edge_sect.at[first, 1], 2 * first, sect_down)
-        send(stage_sect.at[first, 1], edge_sect.at[first, 0], 2 * first, sect_up)
-        send(stage_blk.at[first, 0], edge_blk.at[first, 1], 2 * first + 1, blk_down)
-        send(stage_blk.at[first, 1], edge_blk.at[first, 0], 2 * first + 1, blk_up)
-
-    def take_edges(first):
-        wait_recv(edge_sect.at[first], 2 * first)
-        wait_recv(edge_blk.at[first], 2 * first + 1)
-        sect_low = [jnp.where(sect == 0, 0.0, edge_sect[first, 0, f]) for f in range(count)]
-        sect_high = [jnp.where(sect == n_sect - 1, 0.0, edge_sect[first, 1, f]) for f in range(count)]
-        blk_low = [jnp.where(blk == 0, 0.0, edge_blk[first, 0, r:r + 1, :]) for r in range(2 * count)]
-        blk_high = [jnp.where(blk == n_blk - 1, 0.0, edge_blk[first, 1, r:r + 1, :]) for r in range(2 * count)]
-        return sect_low, sect_high, blk_low, blk_high
+    refined = (jnp.zeros((8, 128), jnp.int32) + levels_ref[0, 0]).astype(F32)
+    for f in range(count):
+        for k in range(2):
+            block[2 * f + k] = cells[f][k]
+            for side, (near, far) in enumerate(((0, 1), (7, 6))):
+                stage_blk[side, k, f:f + 1, :] = cells[f][k][near:near + 1, :]
+                stage_blk[side, 2 + k, f:f + 1, :] = cells[f][k][far:far + 1, :]
+    block[2 * count] = refined
+    for side in range(2):
+        stage_blk[side, 4] = refined
 
     pl.semaphore_wait(barrier, len(peers))
-    send_edges(cells, 0)
-
-    def arrange(low, high, full):
-        wide[low * 16:high * 16, :] = hist[low:high].astype(F32).reshape((high - low) * 16, 128)
-        for q in range(16):
-            snap[low:full, 128 * q:128 * q + 128] = wide[pl.ds(low * 16 + q, full - low, stride=16), :].astype(BF16)
-
+    for side in range(2):
+        send(block, edge_sect.at[1 - side], 0, sect_beside[side])
+        send(stage_blk.at[side], edge_blk.at[1 - side], 1, blk_beside[side])
+        for up in range(2):
+            send(stage_blk.at[up, side], edge_corner.at[1 - side, 1 - up], 2, corners[side][up])
+
+    local = snap.shape[1]
     loads[0].wait()
-    arrange(0, HALF, HALF)
-    first = snap[0:HALF, :]
+    first = hist[0:HALF].reshape(HALF, local)
+    snap[0:HALF, :] = first
     square = dot_rows(first, first)
     third = HALF // 8
     for part in range(3):
@@ -255,8 +237,10 @@
     send(p_send.at[1 - core], p_half, 4, other)
 
     loads[2].wait()
-    arrange(HALF, stored, columns)
-    second = snap[HALF:columns, :]
+    second = jnp.concatenate(
+        [hist[HALF:stored].reshape(stored - HALF, local), jnp.zeros((2 * count, local), BF16)], axis=0
+    )
+    snap[HALF:columns, :] = second
     h_send[0] = dot_rows(first, second).reshape(RING, 16, 128)
     h_send[1] = dot_rows(second, second).reshape(RING, 16, 128)
     send(h_send.at[1 - core], h_half.at[0], 5, other)
@@ -264,7 +248,7 @@
     def p_phase(phase):
         for k in range(RING - 1):
             for part in range(3):
-                send(p_part.at[phase, part], p_slots.at[phase, part, k], 6 + phase, along[(part + phase) % 3][k])
+                send(p_part.at[phase, part], p_slots.at[phase, part, k], 6 + phase, over[(part + phase) % 3][k])
 
     def p_sum(phase):
         wait_recv(p_slots.at[phase], 6 + phase)
@@ -285,53 +269,99 @@
     wait_recv(h_half.at[0], 5)
     h_half[1] = h_send[core] + h_half[0]
     for k in range(1, RING):
-        send(h_half.at[1, (y + k) % RING], h_slots.at[0, k - 1], 9, along_y[k - 1])
+        send(h_half.at[1, (y + k) % RING], h_slots.at[0, k - 1], 9, over_y[k - 1])
+
+    p_part[1] = p_sum(0)
+    p_phase(1)
+
+    wait_recv(h_slots.at[0], 9)
+    h_part[0] = total_of(h_half[1, y], h_slots[0])
+    for k in range(1, RING):
+        send(h_part.at[0], h_slots.at[1, k - 1], 10, over_x[k - 1])
 
     for load in loads[3:]:
         load.wait()
-    refined = (jnp.zeros((8, 128), jnp.int32) + levels_ref[0, 0]).astype(F32)
-    stride = 1.0 / (1.0 + refined)
     diffusivity = [jnp.broadcast_to(diff[0:1, f:f + 1], (8, 128)) for f in range(count)]
     coupling = {
         (f, g): jnp.broadcast_to(coup[f:f + 1, g:g + 1], (8, 128)) for f in range(count) for g in range(count)
     }
-    beside = neighbour_sum(cells, *take_edges(0), sub, lane)
-    tend = tendency(cells, beside, diffusivity, coupling)
-    first_state = [[cells[f][k] + stride * tend[f][k] for k in range(2)] for f in range(count)]
-    send_edges(first_state, 1)
-
-    p_part[1] = p_sum(0)
-    p_phase(1)
-
-    wait_recv(h_slots.at[0], 9)
-    h_part[0] = total_of(h_half[1, y], h_slots[0])
-    for k in range(1, RING):
-        send(h_part.at[0], h_slots.at[1, k - 1], 10, along_x[k - 1])
-
-    p_part[2] = p_sum(1)
-    p_phase(2)
-
-    wait_recv(h_slots.at[1], 10)
-    h_part[1] = total_of(h_part[0], h_slots[1])
-    for k in range(1, RING):
-        send(h_part.at[1], h_slots.at[2, k - 1], 11, along_z[k - 1])
-
-    beside = neighbour_sum(first_state, *take_edges(1), sub, lane)
-    tend = tendency(first_state, beside, diffusivity, coupling)
+    spare = [jnp.zeros((8 - count, 128), F32)]
+    diffusivity_rows = jnp.concatenate([diffusivity[f][0:1] for f in range(count)] + spare, axis=0)
+    coupling_rows = [
+        jnp.concatenate([coupling[f, g][0:1] for f in range(count)] + spare, axis=0) for g in range(count)
+    ]
+    wait_recv(edge_sect, 0)
+    wait_recv(edge_blk, 1)
+    wait_recv(edge_corner, 2)
+    sect_out = [sect == 0, sect == n_sect - 1]
+    blk_out = [blk == 0, blk == n_blk - 1]
+
+    def inside(out, value):
+        return jnp.where(out, 0.0, value)
+
+    corner_rows = [
+        [inside(sect_out[a] | blk_out[b], edge_corner[a, b]) for b in range(2)] for a in range(2)
+    ]
+    near = [[inside(blk_out[b], edge_blk[b, k]) for k in range(2)] for b in range(2)]
+    far = [[inside(blk_out[b], edge_blk[b, 2 + k]) for k in range(2)] for b in range(2)]
+    slabs = [
+        [inside(sect_out[0], edge_sect[0, 2 * f]) for f in range(count)],
+        [inside(sect_out[0], edge_sect[0, 2 * f + 1]) for f in range(count)],
+        [cells[f][0] for f in range(count)],
+        [cells[f][1] for f in range(count)],
+        [inside(sect_out[1], edge_sect[1, 2 * f]) for f in range(count)],
+        [inside(sect_out[1], edge_sect[1, 2 * f + 1]) for f in range(count)],
+    ]
+    strides = [1.0 / (1.0 + edge_sect[0, 2 * count]), None, None, 1.0 / (1.0 + edge_sect[1, 2 * count])]
+    stride = 1.0 / (1.0 + refined)
+    strides[1] = strides[2] = stride
+    low_rows = [corner_rows[0][0], near[0][0], near[0][1], corner_rows[1][0]]
+    high_rows = [corner_rows[0][1], near[1][0], near[1][1], corner_rows[1][1]]
+    first_slabs = []
+    for n in range(4):
+        slab = slabs[n + 1]
+        beside = [
+            slabs[n][f] + slabs[n + 2][f] + along_z(slab[f], lane)
+            + along_y(slab[f], low_rows[n][f:f + 1], high_rows[n][f:f + 1], sub)
+            for f in range(count)
+        ]
+        tend = slab_tendency(slab, beside, diffusivity, coupling)
+        first_slabs.append([slab[f] + strides[n] * tend[f] for f in range(count)])
+    first_slabs[0] = [inside(sect_out[0], tile) for tile in first_slabs[0]]
+    first_slabs[3] = [inside(sect_out[1], tile) for tile in first_slabs[3]]
+    first_rows = []
+    for b in range(2):
+        stride_rows = 1.0 / (1.0 + edge_blk[b, 4])
+        beside_rows = [corner_rows[0][b], near[b][0], near[b][1], corner_rows[1][b]]
+        sides = []
+        for k in range(2):
+            rows = near[b][k]
+            beside = beside_rows[k] + beside_rows[k + 2] + far[b][k] + stage_blk[b, k] + along_z(rows, lane)
+            tend = diffusivity_rows * (beside - 6.0 * rows)
+            for g in range(count):
+                tend = tend + coupling_rows[g] * jnp.broadcast_to(rows[g:g + 1], (8, 128))
+            sides.append(inside(blk_out[b], rows + stride_rows * tend))
+        first_rows.append(sides)
+
     weight = refined * stride
-    for f in range(count):
-        for k in range(2):
-            final = first_state[f][k] + weight * tend[f][k]
-            row = (stored + f) * 16 + 8 * k
-            wide[row:row + 8, :] = final
-            row = (stored + count + f) * 16 + 8 * k
-            wide[row:row + 8, :] = final - cells[f][k]
-    for q in range(16):
-        high, mid, low = split3(wide[pl.ds((columns - TAIL) * 16 + q, TAIL, stride=16), :])
-        snap[columns - TAIL:columns, 128 * q:128 * q + 128] = high
-        fine[0, :, 128 * q:128 * q + 128] = mid
-        fine[1, :, 128 * q:128 * q + 128] = low
-    pieces = jnp.concatenate([snap[columns - TAIL:columns, :], fine[0], fine[1]], axis=0)
+    for k in range(2):
+        slab = first_slabs[k + 1]
+        beside = [
+            first_slabs[k][f] + first_slabs[k + 2][f] + along_z(slab[f], lane)
+            + along_y(slab[f], first_rows[0][k][f:f + 1], first_rows[1][k][f:f + 1], sub)
+            for f in range(count)
+        ]
+        tend = slab_tendency(slab, beside, diffusivity, coupling)
+        for f in range(count):
+            final = slab[f] + weight * tend[f]
+            newest[TAIL - 2 * count + f, k] = final
+            newest[TAIL - count + f, k] = final - cells[f][k]
+    newest[0:TAIL - 2 * count] = hist[columns - TAIL:stored].astype(F32)
+    high, mid, low = split3(newest[...].reshape(TAIL, local))
+    snap[columns - TAIL:columns, :] = high
+    fine[0] = mid
+    fine[1] = low
+    pieces = jnp.concatenate([high, mid, low], axis=0)
     fresh = dot_rows(pieces, snap[...])
     fresh_fine = dot_rows(pieces, pieces[TAIL:])
     fresh = fresh[0:TAIL] + fresh[TAIL:2 * TAIL] + fresh[2 * TAIL:]
@@ -344,7 +374,20 @@
     wait_recv(f_half.at[0], 12)
     f_part[0] = f_send[core] + f_half[0]
     for k in range(1, RING):
-        send(f_part.at[0], f_slots.at[0, k - 1], 13, along_x[k - 1])
+        send(f_part.at[0], f_slots.at[0, k - 1], 13, over_y[k - 1])
+
+    p_part[2] = p_sum(1)
+    p_phase(2)
+
+    wait_recv(h_slots.at[1], 10)
+    h_part[1] = total_of(h_part[0], h_slots[1])
+    for k in range(1, RING):
+        send(h_part.at[1], h_slots.at[2, k - 1], 11, over_z[k - 1])
+
+    wait_recv(f_slots.at[0], 13)
+    f_part[1] = total_of(f_part[0], f_slots[0])
+    for k in range(1, RING):
+        send(f_part.at[1], f_slots.at[1, k - 1], 16, over_x[k - 1])
 
     p_final[core] = p_sum(2)
     send(p_final.at[core], p_final.at[core], 14, other)
@@ -352,7 +395,7 @@
     wait_recv(h_slots.at[2], 11)
     h_final[core, y] = total_of(h_part[1], h_slots[2])
     for k in range(1, RING):
-        send(h_final.at[core, y], h_final.at[core, y], 15, along_y[k - 1])
+        send(h_final.at[core, y], h_final.at[core, y], 15, over_y[k - 1])
 
     wait_recv(p_final.at[0], 14)
 
@@ -376,19 +419,15 @@
 
     def between_first(index):
         if index == 1:
-            wait_recv(f_slots.at[0], 13)
-            f_part[1] = total_of(f_part[0], f_slots[0])
+            wait_recv(f_slots.at[1], 16)
+            f_part[2] = total_of(f_part[1], f_slots[1])
             for k in range(1, RING):
-                send(f_part.at[1], f_slots.at[1, k - 1], 16, along_z[k - 1])
+                send(f_part.at[2], f_slots.at[2, k - 1], 18, over_z[k - 1])
 
     eliminate_half(work, [32, 64, 96, 128], store_first, between_first)
 
     wait_recv(h_slots.at[2], 15)
     send(h_final.at[core], h_final.at[core], 17, other)
-    wait_recv(f_slots.at[1], 16)
-    f_part[2] = total_of(f_part[1], f_slots[1])
-    for k in range(1, RING):
-        send(f_part.at[2], f_slots.at[2, k - 1], 18, along_y[k - 1])
     wait_recv(h_final.at[0], 17)
 
     solved = inverse_ref[0:HALF, 0:HALF]
@@ -440,9 +479,9 @@
         col >= row + (HALF - TAIL), done[:, :HALF] * (1.0 / scale), 0.0
     )
 
-    for round_ in range(2):
-        wait_send(edge_sect.at[round_], 2 * round_)
-        wait_send(edge_blk.at[round_], 2 * round_ + 1)
+    wait_send(edge_sect, 0)
+    wait_send(edge_blk, 1)
+    wait_send(edge_corner, 2)
     wait_send(p_half, 4)
     wait_send(h_half.at[0], 5)
     for phase in range(3):
@@ -468,20 +507,21 @@
     scale = math.sqrt(total_rows)
     keep = pltpu.make_async_copy(upper_ref, factor_ref, local_sem.at[0])
     keep.start()
-    step = 64
+    step = 128
     stores = []
     tail = jnp.concatenate([fine[0], fine[0], fine[0], fine[1]], axis=0)
     for r0 in range(0, size, step):
         h, m, l = split3(inverse_ref[r0:r0 + step, :] * scale)
-        out = jnp.dot(h, snap[...], preferred_element_type=F32)
-        out = out + jnp.dot(m, snap[...], preferred_element_type=F32)
-        out = out + jnp.dot(l, snap[...], preferred_element_type=F32)
+        left = jnp.concatenate([h, m, l], axis=0)
         last = jnp.concatenate(
             [h[:, size - TAIL:], m[:, size - TAIL:], l[:, size - TAIL:], h[:, size - TAIL:]], axis=1
         )
-        out = out + jnp.dot(last, tail, preferred_element_type=F32)
-        for q in range(16):
-            modes[pl.ds(r0 * 16 + q, step, stride=16), :] = out[:, 128 * q:128 * q + 128]
+        for c in range(0, snap.shape[1], 256):
+            out = jnp.dot(left, snap[:, c:c + 256], preferred_element_type=F32)
+            out = (out[:step] + out[step:2 * step]) + out[2 * step:]
+            out = out + jnp.dot(last, tail[:, c:c + 256], preferred_element_type=F32)
+            for q in range(2):
+                modes[pl.ds(r0 * 16 + c // 128 + q, step, stride=16), :] = out[:, 128 * q:128 * q + 128]
         store = pltpu.make_async_copy(
             modes.at[pl.ds(r0 * 16, step * 16)], modes_ref.at[pl.ds(r0 * 16, step * 16)], local_sem.at[1 + r0 // step]
         )
@@ -519,14 +559,15 @@
         out_specs=[vmem, vmem, vmem, vmem],
         scratch_shapes=[
             pltpu.VMEM(history.shape, BF16),
-            pltpu.VMEM((columns * 16, 128), F32),
+            pltpu.VMEM((TAIL,) + history.shape[1:], F32),
             pltpu.VMEM(fields.shape, F32),
             pltpu.VMEM((1, count), F32),
             pltpu.VMEM((count, count), F32),
-            pltpu.VMEM((2, 2, count, 8, 128), F32),
-            pltpu.VMEM((2, 2, 16, 128), F32),
-            pltpu.VMEM((2, 2, 16, 128), F32),
-            pltpu.VMEM((2, 2, count, 8, 128), F32),
+            pltpu.VMEM((2, 2 * count + 1, 8, 128), F32),
+            pltpu.VMEM((2, 5, 8, 128), F32),
+            pltpu.VMEM((2, 2, 8, 128), F32),
+            pltpu.VMEM((2, 5, 8, 128), F32),
+            pltpu.VMEM((2 * count + 1, 8, 128), F32),
             pltpu.VMEM((2, 3) + tile, F32),
             pltpu.VMEM((3,) + tile, F32),
             pltpu.VMEM((3, 3, RING - 1) + tile, F32),

time: 64.4 us -> 58.8 us (0.913)
  Pallas kernels: 62.9 us -> 57.4 us
    pallas_call x1, Pallas kernels: 59.1 us -> 54.8 us  [shards(): pl.pallas_call(functools.partial(gather_kernel, edges, total_rows), out_s...]
    pallas_call x1, Pallas kernels: 3.83 us -> 2.6 us  [shards(): pl.pallas_call(functools.partial(finish_kernel, total_rows), out_shape=[j...]
where the time goes in v3:
time: 58.8 us; the launch traced here: 58.6 us
  Pallas kernels  57.4 us (98%)
  between operations  1.28 us (2%)
    pallas_call x1, Pallas kernels, shards(): pl.pallas_call(functools.partial(gather_kernel, edges, total_rows), out_s...  54.8 us
    pallas_call x1, Pallas kernels, shards(): pl.pallas_call(functools.partial(finish_kernel, total_rows), out_shape=[j...  2.6 us

profile of v3, /device:TPU:1, one launch (start us, length us, event | category | flops | bytes accessed | tf_op | source)
XLA Modules:
  0.0 58.6 jit_solution(6338562864252161280)
XLA Ops:
  1.3 54.8 %gather.1 = (f32[256,256]{1,0:T(8,128)S(1)}, f32[256,256]{1,0:T(8,128)S(1)}, bf16[256,2048]{1,0:T(8,128)(2,1)S(1)}, bf16[2,16,2048]{2,1,0:T(8,128)(2,1)S(1)}) custom-call(bf16[246,2,8,128]{3,2,1,0:T(8,128)(2,1)} %hist_ref.1, f32[5,2,8,128]{3,2,1,0:T(8,128)} %fields_ref.1, s32[1,1]{1,0:T(1,128)S(6)} %copy.7.levels_ref, f32[1,5]{1,0:T(1,128)} %bitcast.2, ...), custom_call_target="tpu_custom_call" | custom-call | tf_op jit(solution)/shard_map/gather/pallas_call | solution.py:550
  56.0 2.6 %finish.1 = (f32[4096,128]{1,0:T(8,128)}, f32[256,256]{1,0:T(8,128)}) custom-call(f32[256,256]{1,0:T(8,128)S(1)} %get-tuple-element.8.inverse_ref, f32[256,256]{1,0:T(8,128)S(1)} %get-tuple-element.9.upper_ref, bf16[256,2048]{1,0:T(8,128)(2,1)S(1)} %get-tuple-element.10.snap, bf16[2,16,2048]{2,1,0:T(8,128)(2,1)S(1)} %get-tuple-element.11.fine), custom_call_target="tpu_custom_call" | custom-call | tf_op jit(solution)/shard_map/finish/pallas_call | solution.py:597
